TPU v7x, 32 devices: a whole 2x2x4 slice. The times are simulated.
32 devices in a mesh: sub: 8 (over z, y), grp: 4 (over x, core).
Axes of the slice: x: 2, y: 2, z: 4, core: 2. Of those that a mesh axis runs over, the one named last changes fastest.
Arguments:
- residual: float32 [16, 8, 4, 512], P(None, 'sub', 'grp'), may hold values from -6 to 6
- bounds: float32 [2], replicated, may hold values from 0.2 to 14, as said below
- local_inverse: bfloat16 [8, 4, 1024, 1024], P('sub', 'grp'), may hold values from -1 to 2
- corner_basis: bfloat16 [8, 4, 24, 1024], P('sub', 'grp'), may hold values from -1 to 1
- corner_map: int32 [8, 4, 24], P('sub', 'grp'), may hold values from 0 to 31
- coarse_inverse: float32 [32, 32], P(('sub', 'grp')), may hold values from -1 to 2, as said below
Outputs:
- basis: float32 [5, 16, 8, 4, 512], P(None, None, 'sub', 'grp')
- gram: float32 [80, 80], replicated
Inputs may be any that keep to these rules, and one draw needn't show every extreme that they name: bounds[0] lies in 0.2 to 0.4 and bounds[1] in 10 to 14. `coarse_inverse`: symmetric.
All inputs are finite; a program needn't handle non-finite values.
Results may differ from a plain program's by a relative error of at most 0.0022.
Values may be sent and summed in bfloat16 or wider, within the bound.
A program may use at most 64 MiB of HBM per device.

v0:
```python
import jax
import jax.numpy as jnp
from jax import lax
from jax.sharding import PartitionSpec as P

S_STEP = 2
BLOCKS = 5


def passed_along(x, axis, by):
    count = lax.axis_size(axis)
    return lax.ppermute(x, axis, [(i, (i + by) % count) for i in range(count)])


def body(residual, bounds, local_inverse, corner_basis, corner_map, coarse_inverse):
    right_count = residual.shape[0]
    half_width = residual.shape[3]
    face_dofs = half_width // 2
    width = 4 * face_dofs
    first_block = residual.reshape(right_count, half_width)
    inverse = local_inverse.reshape(width, width)
    corners = corner_basis.reshape(-1, width)
    corners_wide = corners.astype(jnp.float32)
    corner_ids = corner_map.reshape(-1)
    coarse_count = coarse_inverse.shape[1]
    corner_table = (
        corner_ids[:, None] == jnp.arange(coarse_count, dtype=jnp.int32)[None, :]
    ).astype(jnp.float32)
    centre_value = (bounds[0] + bounds[1]) / 2.0
    radius_value = (bounds[1] - bounds[0]) / 2.0
    gram_order = BLOCKS * right_count
    full_coarse = lax.all_gather(coarse_inverse, ("sub", "grp"), axis=0, tiled=True)

    def operate(block, gram_part):
        packed = block.astype(jnp.bfloat16)
        up_sub = packed[:, :face_dofs]
        up_grp = packed[:, face_dofs:]
        low_sub = passed_along(up_sub, "sub", 1)
        low_grp = passed_along(up_grp, "grp", 1)
        load_rows = jnp.concatenate([up_sub, -low_sub, up_grp, -low_grp], axis=1)
        local_part = jnp.dot(load_rows, inverse, preferred_element_type=jnp.float32)
        weights = jnp.dot(load_rows, corners.T, preferred_element_type=jnp.float32)
        spread = jnp.dot(weights, corner_table, precision=lax.Precision.HIGHEST)
        reduced = lax.psum(spread, ("sub", "grp"))
        coarse_value = jnp.dot(reduced, full_coarse, precision=lax.Precision.HIGHEST)
        picked = jnp.dot(coarse_value, corner_table.T, precision=lax.Precision.HIGHEST)
        displaced = local_part + jnp.dot(picked, corners_wide, precision=lax.Precision.HIGHEST)
        next_sub = passed_along(displaced[:, face_dofs : 2 * face_dofs], "sub", -1)
        next_grp = passed_along(displaced[:, 3 * face_dofs :], "grp", -1)
        result = jnp.concatenate(
            [
                displaced[:, :face_dofs] - next_sub,
                displaced[:, 2 * face_dofs : 3 * face_dofs] - next_grp,
            ],
            axis=1,
        )
        return (result, gram_part)

    def row_terms(block, basis_store):
        return jnp.dot(
            block, basis_store.reshape(gram_order, half_width).T, precision=lax.Precision.HIGHEST
        )

    basis_store = jnp.zeros((BLOCKS, right_count, half_width), jnp.float32).at[0].set(first_block)
    gram_rows = jnp.zeros((gram_order, gram_order), jnp.float32)
    image, gram_row = operate(first_block, row_terms(first_block, basis_store))
    gram_rows = gram_rows.at[:right_count].set(gram_row)
    second_block = (image - centre_value * first_block) / radius_value
    basis_store = basis_store.at[1].set(second_block)

    def advance(level, carry):
        previous, current, store, rows_sum = carry
        image_now, row_now = operate(current, row_terms(current, store))
        rows_sum = lax.dynamic_update_slice(rows_sum, row_now, (level * right_count, 0))
        following = 2.0 * (image_now - centre_value * current) / radius_value - previous
        store = lax.dynamic_update_slice(store, following[None], (level + 1, 0, 0))
        return (current, following, store, rows_sum)

    previous, current, basis_store, gram_rows = lax.fori_loop(
        1, 2 * S_STEP, advance, (first_block, second_block, basis_store, gram_rows)
    )
    merged = basis_store.reshape(gram_order, half_width)
    scale_value = 1.0 / (half_width * lax.axis_size("sub"))
    gram = lax.psum(jnp.dot(merged, merged.T, precision=lax.Precision.HIGHEST), ("sub", "grp"))
    return (basis_store.reshape(BLOCKS, right_count, 1, 1, half_width), gram * scale_value)


def solution(mesh):
    in_specs = (
        P(None, "sub", "grp", None),
        P(),
        P("sub", "grp", None, None),
        P("sub", "grp", None, None),
        P("sub", "grp", None),
        P(("sub", "grp"), None),
    )
    out_specs = (P(None, None, "sub", "grp", None), P())
    return jax.shard_map(body, mesh=mesh, in_specs=in_specs, out_specs=out_specs, check_vma=False)
```

profile of v0, /device:TPU:0, one launch (start us, length us, event | category | flops | bytes accessed | tf_op | source)
XLA Modules:
  0.0 298.3 jit_solution(3853984938971412881)
XLA Ops:
  0.6 0.0 copy-start.2
  0.7 0.0 copy-start.4
  0.7 0.0 copy-start
  0.7 0.9 copy.19
  1.6 3.0 collective-permute-start.4
  4.6 40.4 %all-gather = f32[32,1,32]{2,1,0:T(1,128)S(1)} all-gather(f32[1,1,32]{2,1,0:T(1,128)} %bitcast.74), channel_id=1, replica_groups=mesh['sub'=8,'grp'=4] {'sub','grp'}, dimensions={0}, use_global_device_ids=true | all-gather | bytes 4224 | tf_op jit(solution)/shard_map/all_gather | solution.py:32
  45.0 0.0 collective-permute-done.4
  45.0 0.0 collective-permute-done.5
  45.0 0.9 fusion.21
  45.9 0.8 fusion.18
  46.8 36.9 %psum.34 = f32[16,32]{1,0:T(8,128)S(1)} all-reduce(f32[16,32]{1,0:T(8,128)S(1)} %fusion.18), channel_id=1, replica_groups=mesh['sub'=8,'grp'=4] {'sub','grp'}, use_global_device_ids=true, to_apply=%region_0.0 | all-reduce | flops 512 | bytes 4096 | tf_op jit(solution)/shard_map/psum | solution.py:44
  83.7 0.1 fusion.35
  83.8 0.9 fusion.17
  84.7 1.0 fusion.24
  85.6 2.0 convolution_add_fusion.1
  87.6 4.0 %collective-permute-start.6 = (f32[16,256]{1,0:T(8,128)S(1)}, f32[16,256]{1,0:T(8,128)S(1)}, u32[]{:S(2)}, u32[]{:S(2)}) collective-permute-start(f32[16,256]{1,0:T(8,128)S(1)} %slice.184), channel_id=1, source_target_pairs={{0,28},{4,0},{8,4},{12,8},{16,12},{20,16},{24,20},{28,24},{1,29},{... | collective-permute-start | bytes 49160 | tf_op jit(solution)/shard_map/ppermute | solution.py:12
  91.6 1.4 collective-permute-done.6
  93.1 0.6 fusion.32
  96.4 159.2 %while.26 = (s32[]{:T(128)}, f32[16,512]{1,0:T(8,128)S(1)}, f32[16,512]{1,0:T(8,128)S(1)}, f32[5,16,512]{2,1,0:T(8,128)S(1)}, bf16[1024,1024]{1,0:T(8,128)(2,1)S...) while((s32[]{:T(128)}, f32[16,512]{1,0:T(8,128)S(1)}, ...), condition=%wide.region_3.4_spmd.clone, body=%wide.region_1.3_spmd.clone.sunk | while | flops 39906820 | bytes 3299887 | solution.py:79
  96.4 0.6 collective-permute-start
  97.0 1.5 collective-permute-start.1
  98.5 1.1 collective-permute-done
  99.6 4.0 %collective-permute-done.1 = bf16[16,256]{1,0:T(8,128)(2,1)S(1)} collective-permute-done((bf16[16,256]{1,0:T(8,128)(2,1)S(1)}, bf16[16,256]{1,0:T(8,128)(2,1)S(1)}, u32[]{:S(2)}, u32[]{:S(2)}) %collective-permute-start.1) | collective-permute-done | bytes 8224 | tf_op jit(solution)/shard_map/while/body/eval_jaxpr/ppermute | solution.py:12
  103.6 0.1 fusion.79
  103.7 0.2 fusion.80
  103.9 37.4 %psum.38 = f32[16,32]{1,0:T(8,128)S(1)} all-reduce(f32[16,32]{1,0:T(8,128)S(1)} %fusion.80), channel_id=1, replica_groups=mesh['sub'=8,'grp'=4] {'sub','grp'}, use_global_device_ids=true, to_apply=%region_2.2 | all-reduce | flops 512 | bytes 4096 | tf_op jit(solution)/shard_map/while/body/eval_jaxpr/psum | solution.py:44
  141.3 0.1 fusion.81
  141.5 0.2 fusion.82
  141.7 0.2 fusion.83
  141.9 0.4 convolution_add_fusion.3
  142.3 3.8 %collective-permute-start.2 = (f32[16,256]{1,0:T(8,128)S(1)}, f32[16,256]{1,0:T(8,128)S(1)}, u32[]{:S(2)}, u32[]{:S(2)}) collective-permute-start(f32[16,256]{1,0:T(8,128)S(1)} %slice.210), channel_id=1, source_target_pairs={{0,28},{4,0},{8,4},{12,8},{16,12},{20,16},{24,20},{28,24},{1,29},{... | collective-permute-start | bytes 49160 | tf_op jit(solution)/shard_map/while/body/eval_jaxpr/ppermute | solution.py:12
  146.1 1.4 collective-permute-done.2
  147.5 1.4 collective-permute-done.3
  149.1 1.4 collective-permute-start
  150.4 2.2 collective-permute-start.1
  152.6 4.4 %collective-permute-done.1 = bf16[16,256]{1,0:T(8,128)(2,1)S(1)} collective-permute-done((bf16[16,256]{1,0:T(8,128)(2,1)S(1)}, bf16[16,256]{1,0:T(8,128)(2,1)S(1)}, u32[]{:S(2)}, u32[]{:S(2)}) %collective-permute-start.1) | collective-permute-done | bytes 8224 | tf_op jit(solution)/shard_map/while/body/eval_jaxpr/ppermute | solution.py:12
  157.0 0.1 fusion.79
  157.2 0.2 fusion.80
  157.4 37.6 %psum.38 = f32[16,32]{1,0:T(8,128)S(1)} all-reduce(f32[16,32]{1,0:T(8,128)S(1)} %fusion.80), channel_id=1, replica_groups=mesh['sub'=8,'grp'=4] {'sub','grp'}, use_global_device_ids=true, to_apply=%region_2.2 | all-reduce | flops 512 | bytes 4096 | tf_op jit(solution)/shard_map/while/body/eval_jaxpr/psum | solution.py:44
  195.0 0.1 fusion.81
  195.1 0.2 fusion.82
  195.3 0.2 fusion.83
  195.5 0.4 convolution_add_fusion.3
  195.9 3.3 %collective-permute-start.2 = (f32[16,256]{1,0:T(8,128)S(1)}, f32[16,256]{1,0:T(8,128)S(1)}, u32[]{:S(2)}, u32[]{:S(2)}) collective-permute-start(f32[16,256]{1,0:T(8,128)S(1)} %slice.210), channel_id=1, source_target_pairs={{0,28},{4,0},{8,4},{12,8},{16,12},{20,16},{24,20},{28,24},{1,29},{... | collective-permute-start | bytes 49160 | tf_op jit(solution)/shard_map/while/body/eval_jaxpr/ppermute | solution.py:12
  199.2 1.4 collective-permute-done.2
  200.7 1.4 collective-permute-done.3
  202.2 1.4 collective-permute-start
  203.6 1.6 collective-permute-start.1
  205.2 0.1 collective-permute-done
  205.3 4.7 %collective-permute-done.1 = bf16[16,256]{1,0:T(8,128)(2,1)S(1)} collective-permute-done((bf16[16,256]{1,0:T(8,128)(2,1)S(1)}, bf16[16,256]{1,0:T(8,128)(2,1)S(1)}, u32[]{:S(2)}, u32[]{:S(2)}) %collective-permute-start.1) | collective-permute-done | bytes 8224 | tf_op jit(solution)/shard_map/while/body/eval_jaxpr/ppermute | solution.py:12
  210.0 0.1 fusion.79
  210.2 0.2 fusion.80
  210.4 38.1 %psum.38 = f32[16,32]{1,0:T(8,128)S(1)} all-reduce(f32[16,32]{1,0:T(8,128)S(1)} %fusion.80), channel_id=1, replica_groups=mesh['sub'=8,'grp'=4] {'sub','grp'}, use_global_device_ids=true, to_apply=%region_2.2 | all-reduce | flops 512 | bytes 4096 | tf_op jit(solution)/shard_map/while/body/eval_jaxpr/psum | solution.py:44
  248.4 0.1 fusion.81
  248.5 0.2 fusion.82
  248.7 0.2 fusion.83
  249.0 0.4 convolution_add_fusion.3
  249.4 3.3 %collective-permute-start.2 = (f32[16,256]{1,0:T(8,128)S(1)}, f32[16,256]{1,0:T(8,128)S(1)}, u32[]{:S(2)}, u32[]{:S(2)}) collective-permute-start(f32[16,256]{1,0:T(8,128)S(1)} %slice.210), channel_id=1, source_target_pairs={{0,28},{4,0},{8,4},{12,8},{16,12},{20,16},{24,20},{28,24},{1,29},{... | collective-permute-start | bytes 49160 | tf_op jit(solution)/shard_map/while/body/eval_jaxpr/ppermute | solution.py:12
  252.6 1.4 collective-permute-done.2
  254.1 1.4 collective-permute-done.3
  255.6 0.8 reshape.122
  256.4 0.3 fusion.36
  256.7 41.0 %psum.35 = f32[80,80]{1,0:T(8,128)S(1)} all-reduce(f32[80,80]{1,0:T(8,128)S(1)} %fusion.36), channel_id=1, replica_groups=mesh['sub'=8,'grp'=4] {'sub','grp'}, use_global_device_ids=true, to_apply=%region_4.5 | all-reduce | flops 6400 | bytes 51200 | tf_op jit(solution)/shard_map/psum | solution.py:84
  297.7 0.6 broadcast_multiply_fusion
  (55 shorter events, 0.3 us)
Async XLA Ops:
  0.6 95.6 %copy-start.1 = (f32[16,1,1,512]{3,2,1,0:T(1,128)S(1)}, f32[16,1,1,512]{3,2,1,0:T(1,128)}, u32[]{:S(2)}) copy-start(f32[16,1,1,512]{3,2,1,0:T(1,128)} %param.12) | copy-start | bytes 98308
  0.6 91.0 %copy-start.2 = (bf16[1,1,24,1024]{3,2,1,0:T(8,128)(2,1)S(1)}, bf16[1,1,24,1024]{3,2,1,0:T(8,128)(2,1)}, u32[]{:S(2)}) copy-start(bf16[1,1,24,1024]{3,2,1,0:T(8,128)(2,1)} %param.15) | copy-start | bytes 147460
  0.7 95.7 %copy-start.4 = (s32[1,1,24]{2,1,0:T(1,128)S(1)}, s32[1,1,24]{2,1,0:T(1,128)}, u32[]{:S(2)}) copy-start(s32[1,1,24]{2,1,0:T(1,128)} %param.16) | copy-start | bytes 292
  0.7 95.7 %copy-start = (bf16[1,1,1024,1024]{3,2,1,0:T(8,128)(2,1)S(1)}, bf16[1,1,1024,1024]{3,2,1,0:T(8,128)(2,1)}, u32[]{:S(2)}) copy-start(bf16[1,1,1024,1024]{3,2,1,0:T(8,128)(2,1)} %param.14) | copy-start | bytes 6291460
  0.7 92.4 %copy-start.3 = (f32[2]{0:T(128)S(1)}, f32[2]{0:T(128)}, u32[]{:S(2)}) copy-start(f32[2]{0:T(128)} %param.13) | copy-start | bytes 28
  1.6 43.4 %collective-permute-start.4 = (bf16[16,256]{1,0:T(8,128)(2,1)S(1)}, bf16[16,256]{1,0:T(8,128)(2,1)S(1)}, u32[]{:S(2)}, u32[]{:S(2)}) collective-permute-start(bf16[16,256]{1,0:T(8,128)(2,1)S(1)} %get-tuple-element.508), channel_id=1, source_target_pairs={{0,4},{4,8},{8,12},{12,16},{16,20},{20,24},{24,28},{28,0},{1,5},{5... | collective-permute-start | bytes 24584 | tf_op jit(solution)/shard_map/ppermute | solution.py:12
  4.6 40.4 %collective-permute-start.5 = (bf16[16,256]{1,0:T(8,128)(2,1)S(1)}, bf16[16,256]{1,0:T(8,128)(2,1)S(1)}, u32[]{:S(2)}, u32[]{:S(2)}) collective-permute-start(bf16[16,256]{1,0:T(8,128)(2,1)S(1)} %get-tuple-element.509), channel_id=1, source_target_pairs={{0,1},{1,2},{2,3},{3,0},{4,5},{5,6},{6,7},{7,4},{8,9},{9,10},{10,1... | collective-permute-start | bytes 24584 | tf_op jit(solution)/shard_map/ppermute | solution.py:12
  87.6 5.5 %collective-permute-start.6 = (f32[16,256]{1,0:T(8,128)S(1)}, f32[16,256]{1,0:T(8,128)S(1)}, u32[]{:S(2)}, u32[]{:S(2)}) collective-permute-start(f32[16,256]{1,0:T(8,128)S(1)} %slice.184), channel_id=1, source_target_pairs={{0,28},{4,0},{8,4},{12,8},{16,12},{20,16},{24,20},{28,24},{1,29},{... | collective-permute-start | bytes 49160 | tf_op jit(solution)/shard_map/ppermute | solution.py:12
  93.1 3.2 %collective-permute-start.7 = (f32[16,256]{1,0:T(8,128)S(1)}, f32[16,256]{1,0:T(8,128)S(1)}, u32[]{:S(2)}, u32[]{:S(2)}) collective-permute-start(f32[16,256]{1,0:T(8,128)S(1)} %get-tuple-element.505), channel_id=1, source_target_pairs={{0,3},{1,0},{2,1},{3,2},{4,7},{5,4},{6,5},{7,6},{8,11},{9,8},{10,9... | collective-permute-start | bytes 49160 | tf_op jit(solution)/shard_map/ppermute | solution.py:12
  96.4 3.1 %collective-permute-start = (bf16[16,256]{1,0:T(8,128)(2,1)S(1)}, bf16[16,256]{1,0:T(8,128)(2,1)S(1)}, u32[]{:S(2)}, u32[]{:S(2)}) collective-permute-start(bf16[16,256]{1,0:T(8,128)(2,1)S(1)} %get-tuple-element.585), channel_id=1, source_target_pairs={{0,1},{1,2},{2,3},{3,0},{4,5},{5,6},{6,7},{7,4},{8,9},{9,10},{10,1... | collective-permute-start | bytes 24584 | tf_op jit(solution)/shard_map/while/body/eval_jaxpr/ppermute | solution.py:12
  97.0 6.6 %collective-permute-start.1 = (bf16[16,256]{1,0:T(8,128)(2,1)S(1)}, bf16[16,256]{1,0:T(8,128)(2,1)S(1)}, u32[]{:S(2)}, u32[]{:S(2)}) collective-permute-start(bf16[16,256]{1,0:T(8,128)(2,1)S(1)} %get-tuple-element.586), channel_id=1, source_target_pairs={{0,4},{4,8},{8,12},{12,16},{16,20},{20,24},{24,28},{28,0},{1,5},{5... | collective-permute-start | bytes 24584 | tf_op jit(solution)/shard_map/while/body/eval_jaxpr/ppermute | solution.py:12
  142.3 5.2 %collective-permute-start.2 = (f32[16,256]{1,0:T(8,128)S(1)}, f32[16,256]{1,0:T(8,128)S(1)}, u32[]{:S(2)}, u32[]{:S(2)}) collective-permute-start(f32[16,256]{1,0:T(8,128)S(1)} %slice.210), channel_id=1, source_target_pairs={{0,28},{4,0},{8,4},{12,8},{16,12},{20,16},{24,20},{28,24},{1,29},{... | collective-permute-start | bytes 49160 | tf_op jit(solution)/shard_map/while/body/eval_jaxpr/ppermute | solution.py:12
  147.5 1.4 collective-permute-start.3
  149.1 3.6 %collective-permute-start = (bf16[16,256]{1,0:T(8,128)(2,1)S(1)}, bf16[16,256]{1,0:T(8,128)(2,1)S(1)}, u32[]{:S(2)}, u32[]{:S(2)}) collective-permute-start(bf16[16,256]{1,0:T(8,128)(2,1)S(1)} %get-tuple-element.585), channel_id=1, source_target_pairs={{0,1},{1,2},{2,3},{3,0},{4,5},{5,6},{6,7},{7,4},{8,9},{9,10},{10,1... | collective-permute-start | bytes 24584 | tf_op jit(solution)/shard_map/while/body/eval_jaxpr/ppermute | solution.py:12
  150.4 6.6 %collective-permute-start.1 = (bf16[16,256]{1,0:T(8,128)(2,1)S(1)}, bf16[16,256]{1,0:T(8,128)(2,1)S(1)}, u32[]{:S(2)}, u32[]{:S(2)}) collective-permute-start(bf16[16,256]{1,0:T(8,128)(2,1)S(1)} %get-tuple-element.586), channel_id=1, source_target_pairs={{0,4},{4,8},{8,12},{12,16},{16,20},{20,24},{24,28},{28,0},{1,5},{5... | collective-permute-start | bytes 24584 | tf_op jit(solution)/shard_map/while/body/eval_jaxpr/ppermute | solution.py:12
  195.9 4.7 %collective-permute-start.2 = (f32[16,256]{1,0:T(8,128)S(1)}, f32[16,256]{1,0:T(8,128)S(1)}, u32[]{:S(2)}, u32[]{:S(2)}) collective-permute-start(f32[16,256]{1,0:T(8,128)S(1)} %slice.210), channel_id=1, source_target_pairs={{0,28},{4,0},{8,4},{12,8},{16,12},{20,16},{24,20},{28,24},{1,29},{... | collective-permute-start | bytes 49160 | tf_op jit(solution)/shard_map/while/body/eval_jaxpr/ppermute | solution.py:12
  200.7 1.4 collective-permute-start.3
  202.2 3.1 %collective-permute-start = (bf16[16,256]{1,0:T(8,128)(2,1)S(1)}, bf16[16,256]{1,0:T(8,128)(2,1)S(1)}, u32[]{:S(2)}, u32[]{:S(2)}) collective-permute-start(bf16[16,256]{1,0:T(8,128)(2,1)S(1)} %get-tuple-element.585), channel_id=1, source_target_pairs={{0,1},{1,2},{2,3},{3,0},{4,5},{5,6},{6,7},{7,4},{8,9},{9,10},{10,1... | collective-permute-start | bytes 24584 | tf_op jit(solution)/shard_map/while/body/eval_jaxpr/ppermute | solution.py:12
  203.6 6.4 %collective-permute-start.1 = (bf16[16,256]{1,0:T(8,128)(2,1)S(1)}, bf16[16,256]{1,0:T(8,128)(2,1)S(1)}, u32[]{:S(2)}, u32[]{:S(2)}) collective-permute-start(bf16[16,256]{1,0:T(8,128)(2,1)S(1)} %get-tuple-element.586), channel_id=1, source_target_pairs={{0,4},{4,8},{8,12},{12,16},{16,20},{20,24},{24,28},{28,0},{1,5},{5... | collective-permute-start | bytes 24584 | tf_op jit(solution)/shard_map/while/body/eval_jaxpr/ppermute | solution.py:12
  249.4 4.7 %collective-permute-start.2 = (f32[16,256]{1,0:T(8,128)S(1)}, f32[16,256]{1,0:T(8,128)S(1)}, u32[]{:S(2)}, u32[]{:S(2)}) collective-permute-start(f32[16,256]{1,0:T(8,128)S(1)} %slice.210), channel_id=1, source_target_pairs={{0,28},{4,0},{8,4},{12,8},{16,12},{20,16},{24,20},{28,24},{1,29},{... | collective-permute-start | bytes 49160 | tf_op jit(solution)/shard_map/while/body/eval_jaxpr/ppermute | solution.py:12
  254.1 1.4 collective-permute-start.3
where the time goes:
time: 299 us; the launch traced here: 298 us
  blocking collectives  231 us (77%)
  starting transfers between devices  25.9 us (9%)
  waiting for transfers between devices  24.4 us (8%)
  matrix products  9.78 us (3%)
  between operations  3.4 us (1%)
    psum x4, blocking collectives, operate(): reduced = lax.psum(spread, ('sub', 'grp'))  150 us
    psum x1, blocking collectives, body(): lax.psum(jnp.dot(merged, merged.T, precision=lax.Precision.HIGHEST), ('su...  41 us
    all_gather x1, blocking collectives, body(): lax.all_gather(coarse_inverse, ('sub', 'grp'), axis=0, tiled=True)  40.4 us
    ppermute x16, starting transfers between devices, passed_along(): return lax.ppermute(x, axis, [(i, (i + by) % count) for i in range(count)])  25.9 us
    ppermute x16, waiting for transfers between devices, passed_along(): return lax.ppermute(x, axis, [(i, (i + by) % count) for i in range(count)])  24.4 us
  transfers between devices with their start and end apart: 16, of which 12 were waited for; matrix products, arithmetic and copies ran while one was open for 0% of the time, Pallas kernels for 0%

commit v1 on v0

v1 whole, which is shorter than its diff:
```python
import functools

import jax
import jax.numpy as jnp
from jax import lax
from jax.experimental import pallas as pl
from jax.experimental.pallas import tpu as pltpu
from jax.sharding import PartitionSpec as P

S_STEP = 2
BLOCKS = 2 * S_STEP + 1
LEVELS = 2 * S_STEP
MESH = pl.DeviceIdType.MESH
HIGHEST = lax.Precision.HIGHEST


def exact(a, b):
    return jnp.dot(a, b, precision=HIGHEST, preferred_element_type=jnp.float32)


def across_rows(a, b, precision=None):
    return lax.dot_general(
        a, b, (((1,), (1,)), ((), ())), precision=precision, preferred_element_type=jnp.float32
    )


def dot(a, b):
    return jnp.dot(a, b, preferred_element_type=jnp.float32)


def kernel(
    nsub, ngrp, inner,
    bounds_ref, res_ref, inv_hbm, corner_ref, map_ref, coarse_ref,
    basis_ref, gram_ref,
    inv, up_out, up_in, low_out, low_in, term_out, term_in, rows_c, near, far, load_w, vec, lift,
    inv_sem, up_send, up_recv, low_send, low_recv, term_send, term_recv,
    rows_send, rows_recv, near_send, near_recv, far_send, far_recv,
):
    right, half = up_out.shape[2], vec.shape[1]
    face = half // 2
    order = BLOCKS * right
    nco = coarse_ref.shape[1]
    planes = nsub // inner
    members = inner * ngrp
    sub = lax.axis_index("sub")
    grp = lax.axis_index("grp")
    plane = lax.div(sub, inner)
    within = lax.rem(sub, inner)
    member = within * ngrp + grp
    next_sub = (lax.rem(sub + 1, nsub), grp)
    prev_sub = (lax.rem(sub + nsub - 1, nsub), grp)
    next_grp = (sub, lax.rem(grp + 1, ngrp))
    prev_grp = (sub, lax.rem(grp + ngrp - 1, ngrp))

    def near_peer(offset):
        other = lax.rem(member + offset, members)
        return (plane * inner + lax.div(other, ngrp), lax.rem(other, ngrp))

    def far_peer(offset):
        return (lax.rem(plane + offset, planes) * inner + within, grp)

    near_peers = [near_peer(o) for o in range(1, members)]
    far_peers = [far_peer(o) for o in range(1, planes)]

    barrier = pltpu.get_barrier_semaphore()
    greeted = near_peers + far_peers + [next_sub, prev_sub]
    for peer in greeted:
        pl.semaphore_signal(barrier, inc=1, device_id=peer, device_id_type=MESH)
    load_inv = pltpu.make_async_copy(inv_hbm.at[0, 0], inv, inv_sem)
    load_inv.start()

    def send(src, dst, send_sem, recv_sem, peer):
        copy = pltpu.make_async_remote_copy(
            src_ref=src, dst_ref=dst, send_sem=send_sem, recv_sem=recv_sem,
            device_id=peer, device_id_type=MESH,
        )
        copy.start()
        return copy

    centre = (bounds_ref[0] + bounds_ref[1]) / 2.0
    radius = (bounds_ref[1] - bounds_ref[0]) / 2.0
    scale = 1.0 / jnp.full((right, half), radius, jnp.float32)
    x = res_ref[:, 0, 0, :]
    vec[...] = jnp.zeros_like(vec)
    load_w[...] = jnp.zeros_like(load_w)
    lift[...] = jnp.zeros_like(lift)
    corners = corner_ref[0, 0]
    ids = map_ref[0]
    table = (lax.broadcasted_iota(jnp.int32, (nco, ids.shape[1]), 0) == ids).astype(jnp.bfloat16)
    terms = dot(table, corners)
    term_out[0] = terms[:, face : 2 * face]
    term_out[1] = terms[:, 3 * face :]
    rows_c[plane, member] = coarse_ref[...]

    def all_but_one(buf, count):
        return buf.at[pl.ds(0, count - 1)]

    def drain(ref, send_sem, recv_sem, peer):
        return pltpu.make_async_remote_copy(
            src_ref=ref, dst_ref=ref, send_sem=send_sem, recv_sem=recv_sem,
            device_id=peer, device_id_type=MESH,
        )

    pending = []

    def start_near(level, message):
        near[level, member] = message
        for peer in near_peers:
            own = near.at[level, member]
            send(own, own, near_send.at[level], near_recv.at[level], peer)

    def pass_far(level):
        landed = drain(all_but_one(near.at[level], members), near_send.at[level], near_recv.at[level], near_peers[0])
        landed.wait_recv()
        pending.append(landed)
        total = near[level, 0]
        for i in range(1, members):
            total = total + near[level, i]
        far[level, plane] = total
        for peer in far_peers:
            own = far.at[level, plane]
            send(own, own, far_send.at[level], far_recv.at[level], peer)

    def finish(level):
        landed = drain(all_but_one(far.at[level], planes), far_send.at[level], far_recv.at[level], far_peers[0])
        landed.wait_recv()
        pending.append(landed)
        total = far[level, 0]
        for i in range(1, planes):
            total = total + far[level, i]
        return total

    pl.semaphore_wait(barrier, len(greeted))

    gram_rows = []
    previous = None
    for level in range(LEVELS):
        packed = x.astype(jnp.bfloat16)
        x_sub, x_grp = packed[:, :face], packed[:, face:]
        up_out[level, 0] = x_sub
        up_out[level, 1] = x_grp
        ups = [
            send(up_out.at[level, d], up_in.at[level, d], up_send.at[level, d], up_recv.at[level, d], peer)
            for d, peer in enumerate((next_sub, next_grp))
        ]
        pending += ups
        if level == 0:
            term_copies = [
                send(term_out.at[d], term_in.at[d], term_send.at[d], term_recv.at[d], peer)
                for d, peer in enumerate((prev_sub, prev_grp))
            ]
            pending += term_copies
            for peer in near_peers:
                own = rows_c.at[plane, member]
                send(own, own, rows_send.at[0], rows_recv.at[0], peer)
        basis_ref[level, :, 0, 0, :] = x
        vec[pl.ds(level * right, right), :] = x

        def message():
            return (
                across_rows(packed, load_w[0])
                + across_rows(packed, load_w[1])
                + across_rows(x, vec[...], HIGHEST)
            )

        if level > 0:
            start_near(level, message())
        else:
            load_inv.wait()
        own = dot(x_sub, inv[:face, :]) + dot(x_grp, inv[2 * face : 3 * face, :])
        for copy in ups:
            copy.wait_recv()
        low_sub = up_in[level, 0]
        low_grp = up_in[level, 1]

        def displaced(first):
            columns = slice(first, first + face)
            return (
                own[:, columns]
                - dot(low_sub, inv[face : 2 * face, columns])
                - dot(low_grp, inv[3 * face :, columns])
            )

        low_out[level, 0] = displaced(face)
        low_out[level, 1] = displaced(3 * face)
        lows = [
            send(low_out.at[level, d], low_in.at[level, d], low_send.at[level, d], low_recv.at[level, d], peer)
            for d, peer in enumerate((prev_sub, prev_grp))
        ]
        pending += lows
        if level == 0:
            for copy in term_copies:
                copy.wait_recv()
            rows = slice(order, order + nco)
            weight = jnp.concatenate(
                [terms[:, :face] - term_in[0], terms[:, 2 * face : 3 * face] - term_in[1]], axis=1
            )
            rough = weight.astype(jnp.bfloat16)
            load_w[0, rows, :] = rough
            load_w[1, rows, :] = (weight - rough.astype(jnp.float32)).astype(jnp.bfloat16)
            start_near(level, message())
            landed = drain(all_but_one(rows_c.at[plane], members), rows_send.at[0], rows_recv.at[0], near_peers[0])
            landed.wait_recv()
            pending.append(landed)
            for peer in far_peers:
                mine = rows_c.at[plane]
                send(mine, mine, rows_send.at[1], rows_recv.at[1], peer)
        up = jnp.concatenate([displaced(0), displaced(2 * face)], axis=1)
        pass_far(level)
        if level == 0:
            landed = drain(all_but_one(rows_c, planes), rows_send.at[1], rows_recv.at[1], far_peers[0])
            landed.wait_recv()
            pending.append(landed)
            lift[rows, :] = exact(rows_c[...].reshape(nco, nco), weight)
        total = finish(level)
        gram_rows.append(total)
        image = up + exact(total, lift[...])
        for copy in lows:
            copy.wait_recv()
        image = image - jnp.concatenate([low_in[level, 0], low_in[level, 1]], axis=1)
        if level == 0:
            following = (image - centre * x) * scale
        else:
            following = 2.0 * (image - centre * x) * scale - previous
        previous, x = x, following

    basis_ref[LEVELS, :, 0, 0, :] = x
    vec[pl.ds(LEVELS * right, right), :] = x
    start_near(LEVELS, across_rows(x, vec[...], HIGHEST))
    pass_far(LEVELS)
    gram_rows.append(finish(LEVELS))
    full = jnp.concatenate(gram_rows, axis=0)[:, :order]
    row = lax.broadcasted_iota(jnp.int32, (order, order), 0)
    column = lax.broadcasted_iota(jnp.int32, (order, order), 1)
    below = jnp.where(lax.div(column, right) < lax.div(row, right), full, 0.0)
    same = jnp.where(lax.div(column, right) == lax.div(row, right), full, 0.0)
    gram_ref[...] = (below + same + below.T) * (1.0 / (half * nsub))
    for copy in pending:
        copy.wait_send()


def body(nsub, ngrp, residual, bounds, local_inverse, corner_basis, corner_map, coarse_inverse):
    right, half = residual.shape[0], residual.shape[3]
    face = half // 2
    width = 4 * face
    rows, nco = coarse_inverse.shape
    order = BLOCKS * right
    inner = 1
    while nsub % (2 * inner) == 0 and 2 * inner * ngrp <= nsub // inner:
        inner *= 2
    planes, members = nsub // inner, inner * ngrp
    wide = -(-(order + nco) // 128) * 128
    vmem = pl.BlockSpec(memory_space=pltpu.VMEM)
    dma = pltpu.SemaphoreType.DMA
    f32, bf16 = jnp.float32, jnp.bfloat16
    return pl.pallas_call(
        functools.partial(kernel, nsub, ngrp, inner),
        out_shape=(
            jax.ShapeDtypeStruct((BLOCKS, right, 1, 1, half), f32),
            jax.ShapeDtypeStruct((order, order), f32),
        ),
        in_specs=[
            pl.BlockSpec(memory_space=pltpu.SMEM),
            vmem,
            pl.BlockSpec(memory_space=pl.ANY),
            vmem,
            vmem,
            vmem,
        ],
        out_specs=(vmem, vmem),
        scratch_shapes=[
            pltpu.VMEM((width, width), bf16),
            pltpu.VMEM((LEVELS, 2, right, face), bf16),
            pltpu.VMEM((LEVELS, 2, right, face), bf16),
            pltpu.VMEM((LEVELS, 2, right, face), f32),
            pltpu.VMEM((LEVELS, 2, right, face), f32),
            pltpu.VMEM((2, nco, face), f32),
            pltpu.VMEM((2, nco, face), f32),
            pltpu.VMEM((planes, members, rows, nco), f32),
            pltpu.VMEM((BLOCKS, members, right, wide), f32),
            pltpu.VMEM((BLOCKS, planes, right, wide), f32),
            pltpu.VMEM((2, wide, half), bf16),
            pltpu.VMEM((wide, half), f32),
            pltpu.VMEM((wide, half), f32),
            dma,
            dma((LEVELS, 2)),
            dma((LEVELS, 2)),
            dma((LEVELS, 2)),
            dma((LEVELS, 2)),
            dma((2,)),
            dma((2,)),
            dma((2,)),
            dma((2,)),
            dma((BLOCKS,)),
            dma((BLOCKS,)),
            dma((BLOCKS,)),
            dma((BLOCKS,)),
        ],
        compiler_params=pltpu.CompilerParams(
            collective_id=0, has_side_effects=True, vmem_limit_bytes=48 * 1024 * 1024
        ),
    )(bounds, residual, local_inverse, corner_basis, corner_map, coarse_inverse)


def solution(mesh):
    in_specs = (
        P(None, "sub", "grp", None),
        P(),
        P("sub", "grp", None, None),
        P("sub", "grp", None, None),
        P("sub", "grp", None),
        P(("sub", "grp"), None),
    )
    out_specs = (P(None, None, "sub", "grp", None), P())
    run = functools.partial(body, mesh.shape["sub"], mesh.shape["grp"])
    return jax.shard_map(run, mesh=mesh, in_specs=in_specs, out_specs=out_specs, check_vma=False)
```

time: 299 us -> 58.2 us (0.19)
  blocking collectives: 231 us -> 0 us
  Pallas kernels: 0 us -> 50.8 us
  starting transfers between devices: 25.9 us -> 0 us
  waiting for transfers between devices: 24.4 us -> 0 us
  matrix products: 9.78 us -> 0 us
  local copies, waits for them, and re-layouts: 2.4 us -> 6.39 us
    psum x5 -> x0, blocking collectives: 191 us -> none  [the longest x4 150 us: operate(): reduced = lax.psum(spread, ('sub', 'grp'))]
    pallas_call x0 -> x1, Pallas kernels: none -> 50.8 us  [body(): pl.pallas_call(functools.partial(kernel, nsub, ngrp, inner), out_shape=(j...]
    all_gather x1 -> x0, blocking collectives: 40.4 us -> none  [body(): lax.all_gather(coarse_inverse, ('sub', 'grp'), axis=0, tiled=True)]
    ppermute x16 -> x0, starting transfers between devices: 25.9 us -> none  [passed_along(): return lax.ppermute(x, axis, [(i, (i + by) % count) for i in range(count)])]
    ppermute x16 -> x0, waiting for transfers between devices: 24.4 us -> none  [passed_along(): return lax.ppermute(x, axis, [(i, (i + by) % count) for i in range(count)])]
    dot_general x25 -> x0, matrix products: 9.78 us -> none  [the longest x4 3.16 us: operate(): local_part = jnp.dot(load_rows, inverse, preferred_element_type=jnp.float32)]
    unnamed x12 -> x14, local copies, waits for them, and re-layouts: 0.97 us -> 6.39 us
  transfers between devices with their start and end apart: 16 -> 0, of which waited for: 12 -> 0; matrix products, arithmetic and copies ran while one was open for 0% -> 0% of each run, Pallas kernels for 0% -> 0%
where the time goes in v1:
time: 58.2 us; the launch traced here: 57.9 us
  Pallas kernels  50.8 us (87%)
  local copies, waits for them, and re-layouts  6.39 us (11%)
  between operations  0.65 us (1%)
    pallas_call x1, Pallas kernels, body(): pl.pallas_call(functools.partial(kernel, nsub, ngrp, inner), out_shape=(j...  50.8 us
    unnamed x14, local copies, waits for them, and re-layouts  6.39 us

profile of v1, /device:TPU:0, one launch (start us, length us, event | category | flops | bytes accessed | tf_op | source)
XLA Modules:
  0.0 57.9 jit_solution(12359214051009899092)
XLA Ops:
  0.6 0.0 copy-start
  0.6 1.6 %copy-done = bf16[1,1,1024,1024]{3,2,1,0:T(8,128)(2,1)S(1)} copy-done((bf16[1,1,1024,1024]{3,2,1,0:T(8,128)(2,1)S(1)}, bf16[1,1,1024,1024]{3,2,1,0:T(8,128)(2,1)}, u32[]{:S(2)}) %copy-start) | copy-done | bytes 2097176
  2.2 0.0 copy-start.1
  2.2 0.8 %copy-done.1 = bf16[1,1,24,1024]{3,2,1,0:T(8,128)(2,1)S(1)} copy-done((bf16[1,1,24,1024]{3,2,1,0:T(8,128)(2,1)S(1)}, bf16[1,1,24,1024]{3,2,1,0:T(8,128)(2,1)}, u32[]{:S(2)}) %copy-start.1) | copy-done | bytes 49176
  3.0 0.0 copy-start.2
  3.0 0.8 %copy-done.2 = f32[16,1,1,512]{3,2,1,0:T(1,128)S(1)} copy-done((f32[16,1,1,512]{3,2,1,0:T(1,128)S(1)}, f32[16,1,1,512]{3,2,1,0:T(1,128)}, u32[]{:S(2)}) %copy-start.2) | copy-done | bytes 32792
  3.8 0.0 copy-start.3
  3.8 0.7 %copy-done.3 = f32[2]{0:T(128)S(1)} copy-done((f32[2]{0:T(128)S(1)}, f32[2]{0:T(128)}, u32[]{:S(2)}) %copy-start.3) | copy-done | bytes 32
  4.4 0.0 copy-start.4
  4.4 0.7 %copy-done.4 = s32[1,1,24]{2,1,0:T(1,128)S(1)} copy-done((s32[1,1,24]{2,1,0:T(1,128)S(1)}, s32[1,1,24]{2,1,0:T(1,128)}, u32[]{:S(2)}) %copy-start.4) | copy-done | bytes 120
  5.1 0.0 copy-start.5
  5.1 0.7 %copy-done.5 = f32[1,32]{1,0:T(1,128)S(1)} copy-done((f32[1,32]{1,0:T(1,128)S(1)}, f32[1,32]{1,0:T(1,128)}, u32[]{:S(2)}) %copy-start.5) | copy-done | bytes 152
  5.7 50.8 %shard_map.77 = (f32[5,16,1,1,512]{4,3,2,1,0:T(1,128)S(1)}, f32[80,80]{1,0:T(8,128)S(1)}) custom-call(f32[2]{0:T(128)S(1)} %copy-done.3, f32[16,1,1,512]{3,2,1,0:T(1,128)S(1)} %copy-done.2, bf16[1,1,1024,1024]{3,2,1,0:T(8,128)(2,1)S(1)} %copy-done, bf16[1,1,24,1024]{3,2,1,0:T(8,128)(2,1)S(1)} %copy-done.1, s32[1,1,24]{2,1,0:T(1,128)S(1)} %copy-done.4, ...), custom_call_target="tpu_custom_call" | custom-call | tf_op jit(solution)/shard_map/pallas_call | solution.py:256
  56.6 0.7 %copy.10 = f32[5,16,1,1,512]{4,3,2,1,0:T(1,128)} copy(f32[5,16,1,1,512]{4,3,2,1,0:T(1,128)S(1)} %get-tuple-element.4) | data formatting | bytes 327680
  57.2 0.6 %copy.11 = f32[80,80]{1,0:T(8,128)} copy(f32[80,80]{1,0:T(8,128)S(1)} %get-tuple-element.5) | data formatting | bytes 51200
Async XLA Ops:
  0.6 1.6 %copy-start = (bf16[1,1,1024,1024]{3,2,1,0:T(8,128)(2,1)S(1)}, bf16[1,1,1024,1024]{3,2,1,0:T(8,128)(2,1)}, u32[]{:S(2)}) copy-start(bf16[1,1,1024,1024]{3,2,1,0:T(8,128)(2,1)} %inv_hbm.1) | copy-start | bytes 6291460
  2.2 0.8 %copy-start.1 = (bf16[1,1,24,1024]{3,2,1,0:T(8,128)(2,1)S(1)}, bf16[1,1,24,1024]{3,2,1,0:T(8,128)(2,1)}, u32[]{:S(2)}) copy-start(bf16[1,1,24,1024]{3,2,1,0:T(8,128)(2,1)} %corner_ref.1) | copy-start | bytes 147460
  3.0 0.8 %copy-start.2 = (f32[16,1,1,512]{3,2,1,0:T(1,128)S(1)}, f32[16,1,1,512]{3,2,1,0:T(1,128)}, u32[]{:S(2)}) copy-start(f32[16,1,1,512]{3,2,1,0:T(1,128)} %res_ref.1) | copy-start | bytes 98308
  3.8 0.7 %copy-start.3 = (f32[2]{0:T(128)S(1)}, f32[2]{0:T(128)}, u32[]{:S(2)}) copy-start(f32[2]{0:T(128)} %bounds_ref.1) | copy-start | bytes 28
  4.4 0.7 %copy-start.4 = (s32[1,1,24]{2,1,0:T(1,128)S(1)}, s32[1,1,24]{2,1,0:T(1,128)}, u32[]{:S(2)}) copy-start(s32[1,1,24]{2,1,0:T(1,128)} %map_ref.1) | copy-start | bytes 292
  5.1 0.7 %copy-start.5 = (f32[1,32]{1,0:T(1,128)S(1)}, f32[1,32]{1,0:T(1,128)}, u32[]{:S(2)}) copy-start(f32[1,32]{1,0:T(1,128)} %coarse_ref.1) | copy-start | bytes 388

commit v2 on v1

v2 whole, which is shorter than its diff:
```python
import functools

import jax
import jax.numpy as jnp
from jax import lax
from jax.experimental import pallas as pl
from jax.experimental.pallas import tpu as pltpu
from jax.sharding import PartitionSpec as P

S_STEP = 2
BLOCKS = 2 * S_STEP + 1
LEVELS = 2 * S_STEP
MESH = pl.DeviceIdType.MESH
HIGHEST = lax.Precision.HIGHEST


def exact(a, b):
    return jnp.dot(a, b, precision=HIGHEST, preferred_element_type=jnp.float32)


def across_rows(a, b, precision=None):
    return lax.dot_general(
        a, b, (((1,), (1,)), ((), ())), precision=precision, preferred_element_type=jnp.float32
    )


def dot(a, b):
    return jnp.dot(a, b, preferred_element_type=jnp.float32)


def kernel(
    nsub, ngrp, inner,
    bounds_hbm, res_hbm, inv_hbm, corner_hbm, map_hbm, coarse_hbm,
    basis_hbm, gram_hbm,
    basis_ref, gram_ref, bounds, res, inv, corner, ids_ref, up_out, up_in, low_out, low_in, term_out, term_in, edge,
    rows_c, near, far, high, rest, lift_high, lift_rest,
    load_sem, store_sem, up_send, up_recv, low_send, low_recv, term_send, term_recv, edge_send, edge_recv,
    rows_send, rows_recv, near_send, near_recv, far_send, far_recv,
):
    right, half = up_out.shape[2], high.shape[1]
    face = half // 2
    order = BLOCKS * right
    nco = rows_c.shape[3]
    planes = nsub // inner
    members = inner * ngrp
    sub = lax.axis_index("sub")
    grp = lax.axis_index("grp")
    plane = lax.div(sub, inner)
    within = lax.rem(sub, inner)
    member = within * ngrp + grp
    next_sub = (lax.rem(sub + 1, nsub), grp)
    prev_sub = (lax.rem(sub + nsub - 1, nsub), grp)
    next_grp = (sub, lax.rem(grp + 1, ngrp))
    prev_grp = (sub, lax.rem(grp + ngrp - 1, ngrp))

    def near_peer(offset):
        other = lax.rem(member + offset, members)
        return (plane * inner + lax.div(other, ngrp), lax.rem(other, ngrp))

    def far_peer(offset):
        return (lax.rem(plane + offset, planes) * inner + within, grp)

    near_peers = [near_peer(o) for o in range(1, members)]
    far_peers = [far_peer(o) for o in range(1, planes)]

    barrier = pltpu.get_barrier_semaphore()
    greeted = [next_sub, prev_sub] + far_peers + near_peers
    for peer in greeted:
        pl.semaphore_signal(barrier, inc=1, device_id=peer, device_id_type=MESH)

    loads = [
        pltpu.make_async_copy(src, dst, load_sem.at[i])
        for i, (src, dst) in enumerate((
            (corner_hbm, corner),
            (map_hbm, ids_ref),
            (res_hbm, res),
            (coarse_hbm, rows_c.at[plane, member]),
            (bounds_hbm, bounds),
            (inv_hbm.at[0, 0], inv),
        ))
    ]
    for copy in loads:
        copy.start()

    def send(src, dst, send_sem, recv_sem, peer):
        copy = pltpu.make_async_remote_copy(
            src_ref=src, dst_ref=dst, send_sem=send_sem, recv_sem=recv_sem,
            device_id=peer, device_id_type=MESH,
        )
        copy.start()
        return copy

    pending = []
    stores = []

    def landed(buf, count, send_sem, recv_sem, peer):
        part = buf.at[pl.ds(0, count - 1)]
        copy = pltpu.make_async_remote_copy(
            src_ref=part, dst_ref=part, send_sem=send_sem, recv_sem=recv_sem,
            device_id=peer, device_id_type=MESH,
        )
        copy.wait_recv()
        pending.append(copy)

    def split(value):
        rough = value.astype(jnp.bfloat16)
        return rough, (value - rough.astype(jnp.float32)).astype(jnp.bfloat16)

    def start_near(level, message):
        near[level, member] = message
        own = near.at[level, member]
        for peer in near_peers:
            send(own, own, near_send.at[level], near_recv.at[level], peer)

    def pass_far(level):
        landed(near.at[level], members, near_send.at[level], near_recv.at[level], near_peers[0])
        total = near[level, 0]
        for i in range(1, members):
            total = total + near[level, i]
        far[level, plane] = total
        own = far.at[level, plane]
        for peer in far_peers:
            send(own, own, far_send.at[level], far_recv.at[level], peer)

    def finish(level):
        landed(far.at[level], planes, far_send.at[level], far_recv.at[level], far_peers[0])
        total = far[level, 0]
        for i in range(1, planes):
            total = total + far[level, i]
        return total

    high[...] = jnp.zeros_like(high)
    rest[...] = jnp.zeros_like(rest)
    lift_high[...] = jnp.zeros_like(lift_high)
    lift_rest[...] = jnp.zeros_like(lift_rest)
    loads[0].wait()
    loads[1].wait()
    ids = ids_ref[0]
    table = (lax.broadcasted_iota(jnp.int32, (nco, ids.shape[1]), 0) == ids).astype(jnp.bfloat16)
    terms = dot(table, corner[0, 0])
    term_out[0] = terms[:, face : 2 * face]
    term_out[1] = terms[:, 3 * face :]
    for copy in loads[2:5]:
        copy.wait()
    x = res[:, 0, 0, :]
    centre = (bounds[0] + bounds[1]) / 2.0
    radius = (bounds[1] - bounds[0]) / 2.0
    scale = 1.0 / jnp.full((right, half), radius, jnp.float32)
    lane = lax.broadcasted_iota(jnp.int32, (right, high.shape[0]), 1)
    of_gram = lane < order

    def message(level, packed, remainder):
        both = across_rows(jnp.concatenate([packed, remainder], axis=0), high[...])
        second = across_rows(packed, rest[...])
        return both[:right] + (second + jnp.where(of_gram, both[right:], 0.0))

    def keep(level, value):
        packed, remainder = split(value)
        basis_ref[level, :, 0, 0, :] = value
        stores.append(pltpu.make_async_copy(basis_ref.at[level], basis_hbm.at[level], store_sem.at[level]))
        stores[-1].start()
        high[pl.ds(level * right, right), :] = packed
        rest[pl.ds(level * right, right), :] = remainder
        return packed, remainder

    pl.semaphore_wait(barrier, len(greeted))
    term_copies = [
        send(term_out.at[d], term_in.at[d], term_send.at[d], term_recv.at[d], peer)
        for d, peer in enumerate((prev_sub, prev_grp))
    ]
    pending += term_copies

    gram_rows = []
    previous = None
    for level in range(LEVELS):
        packed = x.astype(jnp.bfloat16)
        x_sub, x_grp = packed[:, :face], packed[:, face:]
        up_out[level, 0] = x_sub
        up_out[level, 1] = x_grp
        ups = [
            send(up_out.at[level, d], up_in.at[level, d], up_send.at[level, d], up_recv.at[level, d], peer)
            for d, peer in enumerate((next_sub, next_grp))
        ]
        pending += ups
        packed, remainder = keep(level, x)
        if level > 0:
            start_near(level, message(level, packed, remainder))
        else:
            own = rows_c.at[plane, member]
            for peer in near_peers:
                send(own, own, rows_send.at[0], rows_recv.at[0], peer)
            loads[5].wait()
            edges = [
                send(
                    inv.at[pl.ds(first, face), pl.ds(first, face)], edge.at[d],
                    edge_send.at[d], edge_recv.at[d], peer,
                )
                for d, (first, peer) in enumerate(((face, prev_sub), (3 * face, prev_grp)))
            ]
            pending += edges

        def own_part(first):
            columns = slice(first, first + face)
            return dot(x_sub, inv[:face, columns]) + dot(x_grp, inv[2 * face : 3 * face, columns])

        def low_part(value, row, first):
            return dot(value, inv[row : row + face, first : first + face])

        def send_low(d, value, peer):
            low_out[level, d] = value
            copy = send(
                low_out.at[level, d], low_in.at[level, d], low_send.at[level, d], low_recv.at[level, d], peer
            )
            pending.append(copy)
            return copy

        own_low = own_part(face)
        ups[1].wait_recv()
        low_grp = up_in[level, 1]
        from_sub = send_low(0, own_low - low_part(low_grp, 3 * face, face), prev_sub)
        own_low = own_part(3 * face)
        up_sub = own_part(0) - low_part(low_grp, 3 * face, 0)
        up_grp = own_part(2 * face) - low_part(low_grp, 3 * face, 2 * face)
        if level == 0:
            for copy in term_copies:
                copy.wait_recv()
            weight = jnp.concatenate(
                [terms[:, :face] - term_in[0], terms[:, 2 * face : 3 * face] - term_in[1]], axis=1
            )
            weight_high, weight_rest = split(weight)
            high[order : order + nco, :] = weight_high
            rest[order : order + nco, :] = weight_rest
            start_near(level, message(level, packed, remainder))
            landed(rows_c.at[plane], members, rows_send.at[0], rows_recv.at[0], near_peers[0])
            mine = rows_c.at[plane]
            for peer in far_peers:
                send(mine, mine, rows_send.at[1], rows_recv.at[1], peer)
        else:
            pass_far(level)
        ups[0].wait_recv()
        low_sub = up_in[level, 0]
        from_grp = send_low(1, own_low - low_part(low_sub, face, 3 * face), prev_grp)
        up_sub = up_sub - low_part(low_sub, face, 0)
        up_grp = up_grp - low_part(low_sub, face, 2 * face)
        if level == 0:
            pass_far(level)
            landed(rows_c, planes, rows_send.at[1], rows_recv.at[1], far_peers[0])
            raised = exact(rows_c[...].reshape(nco, nco), weight)
            raised_high, raised_rest = split(raised)
            lift_high[order : order + nco, :] = raised_high
            lift_rest[order : order + nco, :] = raised_rest
            for copy in edges:
                copy.wait_recv()
        up_sub = up_sub + dot(x_sub, edge[0])
        up_grp = up_grp + dot(x_grp, edge[1])
        base = jnp.concatenate([up_sub, up_grp], axis=1) - centre * x
        total = finish(level)
        gram_rows.append(total)
        total_high, total_rest = split(total)
        both = dot(jnp.concatenate([total_high, total_rest], axis=0), lift_high[...])
        image = base + (both[:right] + (both[right:] + dot(total_high, lift_rest[...])))
        from_sub.wait_recv()
        from_grp.wait_recv()
        image = image - jnp.concatenate([low_in[level, 0], low_in[level, 1]], axis=1)
        following = image * scale if level == 0 else 2.0 * image * scale - previous
        previous, x = x, following

    packed, remainder = keep(LEVELS, x)
    start_near(LEVELS, message(LEVELS, packed, remainder))
    pass_far(LEVELS)
    gram_rows.append(finish(LEVELS))
    full = jnp.concatenate(gram_rows, axis=0)[:, :order]
    row = lax.broadcasted_iota(jnp.int32, (order, order), 0)
    column = lax.broadcasted_iota(jnp.int32, (order, order), 1)
    below = jnp.where(lax.div(column, right) < lax.div(row, right), full, 0.0)
    same = jnp.where(lax.div(column, right) == lax.div(row, right), full, 0.0)
    gram_ref[...] = (below + same + below.T) * (1.0 / (half * nsub))
    stores.append(pltpu.make_async_copy(gram_ref, gram_hbm, store_sem.at[BLOCKS]))
    stores[-1].start()
    for copy in pending:
        copy.wait_send()
    for copy in stores:
        copy.wait()


def body(nsub, ngrp, residual, bounds, local_inverse, corner_basis, corner_map, coarse_inverse):
    right, half = residual.shape[0], residual.shape[3]
    face = half // 2
    width = 4 * face
    rows, nco = coarse_inverse.shape
    order = BLOCKS * right
    inner = 1
    while nsub % (2 * inner) == 0 and 2 * inner * ngrp <= nsub // inner:
        inner *= 2
    planes, members = nsub // inner, inner * ngrp
    wide = -(-(order + nco) // 128) * 128
    hbm = pl.BlockSpec(memory_space=pltpu.HBM)
    dma = pltpu.SemaphoreType.DMA
    f32, bf16 = jnp.float32, jnp.bfloat16
    return pl.pallas_call(
        functools.partial(kernel, nsub, ngrp, inner),
        out_shape=(
            jax.ShapeDtypeStruct((BLOCKS, right, 1, 1, half), f32),
            jax.ShapeDtypeStruct((order, order), f32),
        ),
        in_specs=[hbm] * 6,
        out_specs=(hbm, hbm),
        scratch_shapes=[
            pltpu.VMEM((BLOCKS, right, 1, 1, half), f32),
            pltpu.VMEM((order, order), f32),
            pltpu.SMEM(bounds.shape, f32),
            pltpu.VMEM(residual.shape, f32),
            pltpu.VMEM((width, width), bf16),
            pltpu.VMEM(corner_basis.shape, bf16),
            pltpu.VMEM(corner_map.shape, corner_map.dtype),
            pltpu.VMEM((LEVELS, 2, right, face), bf16),
            pltpu.VMEM((LEVELS, 2, right, face), bf16),
            pltpu.VMEM((LEVELS, 2, right, face), f32),
            pltpu.VMEM((LEVELS, 2, right, face), f32),
            pltpu.VMEM((2, nco, face), f32),
            pltpu.VMEM((2, nco, face), f32),
            pltpu.VMEM((2, face, face), bf16),
            pltpu.VMEM((planes, members, rows, nco), f32),
            pltpu.VMEM((BLOCKS, members, right, wide), f32),
            pltpu.VMEM((BLOCKS, planes, right, wide), f32),
            pltpu.VMEM((wide, half), bf16),
            pltpu.VMEM((wide, half), bf16),
            pltpu.VMEM((wide, half), bf16),
            pltpu.VMEM((wide, half), bf16),
            dma((6,)),
            dma((BLOCKS + 1,)),
            dma((LEVELS, 2)),
            dma((LEVELS, 2)),
            dma((LEVELS, 2)),
            dma((LEVELS, 2)),
            dma((2,)),
            dma((2,)),
            dma((2,)),
            dma((2,)),
            dma((2,)),
            dma((2,)),
            dma((BLOCKS,)),
            dma((BLOCKS,)),
            dma((BLOCKS,)),
            dma((BLOCKS,)),
        ],
        compiler_params=pltpu.CompilerParams(
            collective_id=0, has_side_effects=True, vmem_limit_bytes=60 * 1024 * 1024
        ),
    )(bounds, residual, local_inverse, corner_basis, corner_map, coarse_inverse)


def solution(mesh):
    in_specs = (
        P(None, "sub", "grp", None),
        P(),
        P("sub", "grp", None, None),
        P("sub", "grp", None, None),
        P("sub", "grp", None),
        P(("sub", "grp"), None),
    )
    out_specs = (P(None, None, "sub", "grp", None), P())
    run = functools.partial(body, mesh.shape["sub"], mesh.shape["grp"])
    return jax.shard_map(run, mesh=mesh, in_specs=in_specs, out_specs=out_specs, check_vma=False)
```

time: 58.2 us -> 52.4 us (0.900)
  local copies, waits for them, and re-layouts: 6.39 us -> 2.99 us
  Pallas kernels: 50.8 us -> 48.5 us
    unnamed x14 -> x2, local copies, waits for them, and re-layouts: 6.39 us -> 2.99 us
    pallas_call x1, Pallas kernels: 50.8 us -> 48.5 us  [body(): pl.pallas_call(functools.partial(kernel, nsub, ngrp, inner), out_shape=(j...]
where the time goes in v2:
time: 52.4 us; the launch traced here: 52.2 us
  Pallas kernels  48.5 us (93%)
  local copies, waits for them, and re-layouts  2.99 us (6%)
  between operations  0.64 us (1%)
    pallas_call x1, Pallas kernels, body(): pl.pallas_call(functools.partial(kernel, nsub, ngrp, inner), out_shape=(j...  48.5 us
    unnamed x2, local copies, waits for them, and re-layouts  2.99 us

profile of v2, /device:TPU:0, one launch (start us, length us, event | category | flops | bytes accessed | tf_op | source)
XLA Modules:
  0.0 52.2 jit_solution(17433788518105251398)
XLA Ops:
  0.6 48.5 %shard_map.77 = (f32[5,16,1,1,512]{4,3,2,1,0:T(1,128)}, f32[80,80]{1,0:T(8,128)}) custom-call(f32[2]{0:T(128)} %bounds_hbm.1, f32[16,1,1,512]{3,2,1,0:T(1,128)} %res_hbm.1, bf16[1,1,1024,1024]{3,2,1,0:T(8,128)(2,1)} %inv_hbm.1, bf16[1,1,24,1024]{3,2,1,0:T(8,128)(2,1)} %corner_hbm.1, s32[1,1,24]{2,1,0:T(1,128)} %map_hbm.1, f32[1,32]{1,0:T(1,128)} %coarse_hbm.1), custom_call_target="tpu_custom_call" | custom-call | tf_op jit(solution)/shard_map/pallas_call | solution.py:300
  49.2 1.6 %copy.10 = f32[5,16,1,1,512]{4,3,2,1,0:T(1,128)} copy(f32[5,16,1,1,512]{4,3,2,1,0:T(1,128)} %get-tuple-element.4) | data formatting | bytes 327680
  50.8 1.4 %copy.11 = f32[80,80]{1,0:T(8,128)} copy(f32[80,80]{1,0:T(8,128)} %get-tuple-element.5) | data formatting | bytes 51200

commit v3 on v2

v3 whole, which is shorter than its diff:
```python
import functools

import jax
import jax.numpy as jnp
from jax import lax
from jax.experimental import pallas as pl
from jax.experimental.pallas import tpu as pltpu
from jax.sharding import PartitionSpec as P

S_STEP = 2
BLOCKS = 2 * S_STEP + 1
LEVELS = 2 * S_STEP
MESH = pl.DeviceIdType.MESH
HIGHEST = lax.Precision.HIGHEST


def exact(a, b):
    return jnp.dot(a, b, precision=HIGHEST, preferred_element_type=jnp.float32)


def across_rows(a, b, precision=None):
    return lax.dot_general(
        a, b, (((1,), (1,)), ((), ())), precision=precision, preferred_element_type=jnp.float32
    )


def dot(a, b):
    return jnp.dot(a, b, preferred_element_type=jnp.float32)


def kernel(
    nsub, ngrp, inner, pack,
    bounds_hbm, res_hbm, inv_hbm, corner_hbm, map_hbm, coarse_hbm,
    basis_hbm, gram_hbm,
    basis_ref, gram_ref, bounds, res, inv, corner, ids_ref,
    up_out, up_in, diag_in, low_out, low_in, term_out, term_in, edge, cross,
    rows_c, direct, part_out, part_near, part_far, part_all, near, far,
    high, rest, load_high, load_rest, lift_high, lift_rest,
    load_sem, store_sem, up_send, up_recv, diag_send, diag_recv, low_send, low_recv,
    term_send, term_recv, edge_send, edge_recv, rows_send, rows_recv, direct_send, direct_recv,
    part_send, part_recv, near_send, near_recv, far_send, far_recv,
):
    right, half = up_out.shape[2], high.shape[1]
    face = half // 2
    order = BLOCKS * right
    nco = rows_c.shape[2]
    planes = nsub // inner
    members = inner * ngrp
    devices = nsub * ngrp
    packed_rows = right // pack
    chunk = part_out.shape[1]
    sub = lax.axis_index("sub")
    grp = lax.axis_index("grp")
    me = sub * ngrp + grp
    plane = lax.div(sub, inner)
    within = lax.rem(sub, inner)
    member = within * ngrp + grp
    sub_up, sub_down = lax.rem(sub + 1, nsub), lax.rem(sub + nsub - 1, nsub)
    grp_up, grp_down = lax.rem(grp + 1, ngrp), lax.rem(grp + ngrp - 1, ngrp)
    next_sub, prev_sub = (sub_up, grp), (sub_down, grp)
    next_grp, prev_grp = (sub, grp_up), (sub, grp_down)

    def any_peer(offset):
        other = lax.rem(me + offset, devices)
        return (lax.div(other, ngrp), lax.rem(other, ngrp))

    def to_all(action):
        def step(offset, carry):
            action(any_peer(offset))
            return carry

        lax.fori_loop(1, devices, step, 0)

    near_others = [lax.rem(member + o, members) for o in range(1, members)]
    near_peers = [(plane * inner + lax.div(o, ngrp), lax.rem(o, ngrp)) for o in near_others]
    far_peers = [(lax.rem(plane + o, planes) * inner + within, grp) for o in range(1, planes)]

    barrier = pltpu.get_barrier_semaphore()
    loads = [
        pltpu.make_async_copy(src, dst, load_sem.at[i])
        for i, (src, dst) in enumerate((
            (corner_hbm, corner),
            (map_hbm, ids_ref),
            (res_hbm, res),
            (coarse_hbm, rows_c.at[me]),
            (bounds_hbm, bounds),
            (inv_hbm.at[0, 0], inv),
        ))
    ]
    for copy in loads:
        copy.start()
    to_all(lambda peer: pl.semaphore_signal(barrier, inc=1, device_id=peer, device_id_type=MESH))

    def send(src, dst, send_sem, recv_sem, peer):
        copy = pltpu.make_async_remote_copy(
            src_ref=src, dst_ref=dst, send_sem=send_sem, recv_sem=recv_sem,
            device_id=peer, device_id_type=MESH,
        )
        copy.start()
        return copy

    pending = []
    stores = []

    def landed(buf, count, send_sem, recv_sem, peer):
        part = buf.at[pl.ds(0, count - 1)]
        copy = pltpu.make_async_remote_copy(
            src_ref=part, dst_ref=part, send_sem=send_sem, recv_sem=recv_sem,
            device_id=peer, device_id_type=MESH,
        )
        copy.wait_recv()
        pending.append(copy)

    def split(value):
        rough = value.astype(jnp.bfloat16)
        return rough, (value - rough.astype(jnp.float32)).astype(jnp.bfloat16)

    def added(buf, count):
        total = buf[0]
        for i in range(1, count):
            total = total + buf[i]
        return total

    def broadcast(buf, slot, peers, send_sem, recv_sem):
        own = buf.at[slot]
        for peer in peers:
            send(own, own, send_sem, recv_sem, peer)

    high[...] = jnp.zeros_like(high)
    rest[...] = jnp.zeros_like(rest)
    loads[0].wait()
    loads[1].wait()
    ids = ids_ref[0]
    table = (lax.broadcasted_iota(jnp.int32, (nco, ids.shape[1]), 0) == ids).astype(jnp.bfloat16)
    terms = dot(table, corner[0, 0])
    term_out[0] = terms[:, face : 2 * face]
    term_out[1] = terms[:, 3 * face :]
    for copy in loads[2:5]:
        copy.wait()
    x = res[:, 0, 0, :]
    centre = (bounds[0] + bounds[1]) / 2.0
    radius = (bounds[1] - bounds[0]) / 2.0
    scale = 1.0 / jnp.full((right, half), radius, jnp.float32)
    lane = lax.broadcasted_iota(jnp.int32, (right, pack * nco), 1)
    row = lax.broadcasted_iota(jnp.int32, (right, pack * nco), 0)
    mine = lax.div(lane, nco) == lax.div(row, packed_rows)

    def gram_part(first, second):
        both = across_rows(jnp.concatenate([first, second], axis=0), high[...])
        count = first.shape[0]
        return both[:count] + (both[count:] + across_rows(first, rest[...]))

    def coarse_part(packed):
        part = across_rows(packed, load_high[...]) + across_rows(packed, load_rest[...])
        if pack == 1:
            return part
        part = jnp.where(mine, part, 0.0)
        total = part[:packed_rows]
        for q in range(1, pack):
            total = total + part[q * packed_rows : (q + 1) * packed_rows]
        return total

    def coarse_lift(total):
        if pack > 1:
            total = jnp.where(mine, jnp.concatenate([total] * pack, axis=0), 0.0)
        total_high, total_rest = split(total)
        both = dot(jnp.concatenate([total_high, total_rest], axis=0), lift_high[...])
        return both[:right] + (both[right:] + dot(total_high, lift_rest[...]))

    def send_coarse(level, part):
        direct[level, me] = part
        own = direct.at[level, me]
        to_all(lambda peer: send(own, own, direct_send.at[level], direct_recv.at[level], peer))

    def keep(level, value):
        packed, remainder = split(value)
        basis_ref[level, :, 0, 0, :] = value
        high[pl.ds(level * right, right), :] = packed
        rest[pl.ds(level * right, right), :] = remainder
        stores.append(pltpu.make_async_copy(basis_ref.at[level], basis_hbm.at[level], store_sem.at[level]))
        stores[-1].start()
        return packed, remainder

    pl.semaphore_wait(barrier, devices - 1)
    term_copies = [
        send(term_out.at[d], term_in.at[d], term_send.at[d], term_recv.at[d], peer)
        for d, peer in enumerate((prev_sub, prev_grp))
    ]
    pending += term_copies

    previous = None
    for level in range(LEVELS):
        packed = x.astype(jnp.bfloat16)
        x_sub, x_grp = packed[:, :face], packed[:, face:]
        up_out[level, 0] = x_sub
        up_out[level, 1] = x_grp
        ups = [
            send(up_out.at[level, d], up_in.at[level, d], up_send.at[level, d], up_recv.at[level, d], peer)
            for d, peer in enumerate((next_sub, next_grp))
        ]
        diags = [
            send(up_out.at[level, d], diag_in.at[level, d], diag_send.at[level, d], diag_recv.at[level, d], peer)
            for d, peer in enumerate(((sub_up, grp_down), (sub_down, grp_up)))
        ]
        pending += ups + diags
        if level == 0:
            loads[5].wait()
        else:
            part = coarse_part(packed)

        def own_part(first):
            columns = slice(first, first + face)
            return dot(x_sub, inv[:face, columns]) + dot(x_grp, inv[2 * face : 3 * face, columns])

        def low_part(value, first, column):
            return dot(value, inv[first : first + face, column : column + face])

        low_out[level, 0] = own_part(face)
        low_out[level, 1] = own_part(3 * face)
        lows = [
            send(low_out.at[level, d], low_in.at[level, d], low_send.at[level, d], low_recv.at[level, d], peer)
            for d, peer in enumerate((prev_sub, prev_grp))
        ]
        pending += lows
        if level == 0:
            own = rows_c.at[me]
            to_all(lambda peer: send(own, own, rows_send, rows_recv, peer))
            blocks = [
                send(
                    inv.at[pl.ds(first, face), pl.ds(column, face)], landing.at[d],
                    edge_send.at[i], edge_recv.at[i], peer,
                )
                for i, (first, column, landing, d, peer) in enumerate((
                    (face, face, edge, 0, prev_sub),
                    (3 * face, 3 * face, edge, 1, prev_grp),
                    (3 * face, face, cross, 0, prev_sub),
                    (face, 3 * face, cross, 1, prev_grp),
                ))
            ]
            pending += blocks
            for copy in term_copies:
                copy.wait_recv()
            weight = jnp.concatenate(
                [terms[:, :face] - term_in[0], terms[:, 2 * face : 3 * face] - term_in[1]], axis=1
            )
            weight_high, weight_rest = split(weight)
            load_high[...] = jnp.concatenate([weight_high] * pack, axis=0)
            load_rest[...] = jnp.concatenate([weight_rest] * pack, axis=0)
            part = coarse_part(packed)
        send_coarse(level, part)
        packed, remainder = keep(level, x)
        if level == LEVELS - 1:
            count = LEVELS * right
            first_rows = gram_part(high[:count, :], rest[:count, :])
            for m in range(members):
                part_out[m] = first_rows[m * chunk : (m + 1) * chunk]
            part_near[member] = part_out[member]
            for other, peer in zip(near_others, near_peers):
                send(part_out.at[other], part_near.at[member], part_send.at[0], part_recv.at[0], peer)
        up_sub = own_part(0)
        up_grp = own_part(2 * face)
        for copy in ups:
            copy.wait_recv()
        low_sub, low_grp = up_in[level, 0], up_in[level, 1]
        up_sub = up_sub - low_part(low_sub, face, 0) - low_part(low_grp, 3 * face, 0)
        up_grp = up_grp - low_part(low_sub, face, 2 * face) - low_part(low_grp, 3 * face, 2 * face)
        if level == 0:
            landed(rows_c, devices, rows_send, rows_recv, next_grp)
            raised = exact(rows_c[...].reshape(nco, nco), weight)
            raised_high, raised_rest = split(raised)
            lift_high[...] = jnp.concatenate([raised_high] * pack, axis=0)
            lift_rest[...] = jnp.concatenate([raised_rest] * pack, axis=0)
            for copy in blocks:
                copy.wait_recv()
        up_sub = up_sub + dot(x_sub, edge[0])
        up_grp = up_grp + dot(x_grp, edge[1])
        for copy in diags:
            copy.wait_recv()
        up_sub = up_sub + dot(diag_in[level, 1], cross[0])
        up_grp = up_grp + dot(diag_in[level, 0], cross[1])
        base = jnp.concatenate([up_sub, up_grp], axis=1) - centre * x
        for copy in lows:
            copy.wait_recv()
        base = base - jnp.concatenate([low_in[level, 0], low_in[level, 1]], axis=1)
        landed(direct.at[level], devices, direct_send.at[level], direct_recv.at[level], next_grp)
        image = base + coarse_lift(added(direct.at[level], devices))
        following = image * scale if level == 0 else 2.0 * image * scale - previous
        previous, x = x, following

    packed, remainder = keep(LEVELS, x)
    near[member] = gram_part(packed, remainder)
    broadcast(near, member, near_peers, near_send, near_recv)
    landed(part_near, members, part_send.at[0], part_recv.at[0], near_peers[0])
    part_far[plane] = added(part_near, members)
    broadcast(part_far, plane, far_peers, part_send.at[1], part_recv.at[1])
    landed(near, members, near_send, near_recv, near_peers[0])
    far[plane] = added(near, members)
    broadcast(far, plane, far_peers, far_send, far_recv)
    landed(part_far, planes, part_send.at[1], part_recv.at[1], far_peers[0])
    part_all[member] = added(part_far, planes)
    broadcast(part_all, member, near_peers, part_send.at[2], part_recv.at[2])
    landed(far, planes, far_send, far_recv, far_peers[0])
    last_rows = added(far, planes)
    landed(part_all, members, part_send.at[2], part_recv.at[2], near_peers[0])
    full = jnp.concatenate([part_all[m] for m in range(members)] + [last_rows], axis=0)[:, :order]
    row = lax.broadcasted_iota(jnp.int32, (order, order), 0)
    column = lax.broadcasted_iota(jnp.int32, (order, order), 1)
    below = jnp.where(lax.div(column, right) < lax.div(row, right), full, 0.0)
    same = jnp.where(lax.div(column, right) == lax.div(row, right), full, 0.0)
    gram_ref[...] = (below + same + below.T) * (1.0 / (half * nsub))
    stores.append(pltpu.make_async_copy(gram_ref, gram_hbm, store_sem.at[BLOCKS]))
    stores[-1].start()
    for copy in pending:
        copy.wait_send()
    for copy in stores:
        copy.wait()


def body(nsub, ngrp, residual, bounds, local_inverse, corner_basis, corner_map, coarse_inverse):
    right, half = residual.shape[0], residual.shape[3]
    face = half // 2
    width = 4 * face
    rows, nco = coarse_inverse.shape
    order = BLOCKS * right
    devices = nsub * ngrp
    inner = 1
    while nsub % (2 * inner) == 0 and 2 * inner * ngrp <= nsub // inner:
        inner *= 2
    planes, members = nsub // inner, inner * ngrp
    wide = -(-order // 128) * 128
    pack = 128 // nco if nco < 128 and 128 % nco == 0 and right % (128 // nco) == 0 else 1
    lanes = pack * nco
    chunk = LEVELS * right // members
    hbm = pl.BlockSpec(memory_space=pltpu.HBM)
    dma = pltpu.SemaphoreType.DMA
    f32, bf16 = jnp.float32, jnp.bfloat16
    return pl.pallas_call(
        functools.partial(kernel, nsub, ngrp, inner, pack),
        out_shape=(
            jax.ShapeDtypeStruct((BLOCKS, right, 1, 1, half), f32),
            jax.ShapeDtypeStruct((order, order), f32),
        ),
        in_specs=[hbm] * 6,
        out_specs=(hbm, hbm),
        scratch_shapes=[
            pltpu.VMEM((BLOCKS, right, 1, 1, half), f32),
            pltpu.VMEM((order, order), f32),
            pltpu.SMEM(bounds.shape, f32),
            pltpu.VMEM(residual.shape, f32),
            pltpu.VMEM((width, width), bf16),
            pltpu.VMEM(corner_basis.shape, bf16),
            pltpu.VMEM(corner_map.shape, corner_map.dtype),
            pltpu.VMEM((LEVELS, 2, right, face), bf16),
            pltpu.VMEM((LEVELS, 2, right, face), bf16),
            pltpu.VMEM((LEVELS, 2, right, face), bf16),
            pltpu.VMEM((LEVELS, 2, right, face), f32),
            pltpu.VMEM((LEVELS, 2, right, face), f32),
            pltpu.VMEM((2, nco, face), f32),
            pltpu.VMEM((2, nco, face), f32),
            pltpu.VMEM((2, face, face), bf16),
            pltpu.VMEM((2, face, face), bf16),
            pltpu.VMEM((devices, rows, nco), f32),
            pltpu.VMEM((LEVELS, devices, right // pack, lanes), f32),
            pltpu.VMEM((members, chunk, wide), f32),
            pltpu.VMEM((members, chunk, wide), f32),
            pltpu.VMEM((planes, chunk, wide), f32),
            pltpu.VMEM((members, chunk, wide), f32),
            pltpu.VMEM((members, right, wide), f32),
            pltpu.VMEM((planes, right, wide), f32),
            pltpu.VMEM((wide, half), bf16),
            pltpu.VMEM((wide, half), bf16),
            pltpu.VMEM((lanes, half), bf16),
            pltpu.VMEM((lanes, half), bf16),
            pltpu.VMEM((lanes, half), bf16),
            pltpu.VMEM((lanes, half), bf16),
            dma((6,)),
            dma((BLOCKS + 1,)),
            dma((LEVELS, 2)),
            dma((LEVELS, 2)),
            dma((LEVELS, 2)),
            dma((LEVELS, 2)),
            dma((LEVELS, 2)),
            dma((LEVELS, 2)),
            dma((2,)),
            dma((2,)),
            dma((4,)),
            dma((4,)),
            dma,
            dma,
            dma((LEVELS,)),
            dma((LEVELS,)),
            dma((3,)),
            dma((3,)),
            dma,
            dma,
            dma,
            dma,
        ],
        compiler_params=pltpu.CompilerParams(
            collective_id=0, has_side_effects=True, vmem_limit_bytes=60 * 1024 * 1024
        ),
    )(bounds, residual, local_inverse, corner_basis, corner_map, coarse_inverse)


def solution(mesh):
    in_specs = (
        P(None, "sub", "grp", None),
        P(),
        P("sub", "grp", None, None),
        P("sub", "grp", None, None),
        P("sub", "grp", None),
        P(("sub", "grp"), None),
    )
    out_specs = (P(None, None, "sub", "grp", None), P())
    run = functools.partial(body, mesh.shape["sub"], mesh.shape["grp"])
    return jax.shard_map(run, mesh=mesh, in_specs=in_specs, out_specs=out_specs, check_vma=False)
```

time: 52.4 us -> 47 us (0.90)
  Pallas kernels: 48.5 us -> 43.1 us
    pallas_call x1, Pallas kernels: 48.5 us -> 43.1 us  [body(): pl.pallas_call(functools.partial(kernel, nsub, ngrp, inner, pack), out_sh...]
where the time goes in v3:
time: 47 us; the launch traced here: 46.8 us
  Pallas kernels  43.1 us (92%)
  local copies, waits for them, and re-layouts  2.99 us (6%)
  between operations  0.64 us (1%)
    pallas_call x1, Pallas kernels, body(): pl.pallas_call(functools.partial(kernel, nsub, ngrp, inner, pack), out_sh...  43.1 us
    unnamed x2, local copies, waits for them, and re-layouts  2.99 us

profile of v3, /device:TPU:0, one launch (start us, length us, event | category | flops | bytes accessed | tf_op | source)
XLA Modules:
  0.0 46.8 jit_solution(9193101220452935884)
XLA Ops:
  0.6 43.1 %shard_map.77 = (f32[5,16,1,1,512]{4,3,2,1,0:T(1,128)}, f32[80,80]{1,0:T(8,128)}) custom-call(f32[2]{0:T(128)} %bounds_hbm.1, f32[16,1,1,512]{3,2,1,0:T(1,128)} %res_hbm.1, bf16[1,1,1024,1024]{3,2,1,0:T(8,128)(2,1)} %inv_hbm.1, bf16[1,1,24,1024]{3,2,1,0:T(8,128)(2,1)} %corner_hbm.1, s32[1,1,24]{2,1,0:T(1,128)} %map_hbm.1, f32[1,32]{1,0:T(1,128)} %coarse_hbm.1), custom_call_target="tpu_custom_call" | custom-call | tf_op jit(solution)/shard_map/pallas_call | solution.py:337
  43.8 1.6 %copy.10 = f32[5,16,1,1,512]{4,3,2,1,0:T(1,128)} copy(f32[5,16,1,1,512]{4,3,2,1,0:T(1,128)} %get-tuple-element.4) | data formatting | bytes 327680
  45.4 1.4 %copy.11 = f32[80,80]{1,0:T(8,128)} copy(f32[80,80]{1,0:T(8,128)} %get-tuple-element.5) | data formatting | bytes 51200

commit v4 on v3

--- a/solution.py
+++ b/solution.py
@@ -10,7 +10,7 @@
 S_STEP = 2
 BLOCKS = 2 * S_STEP + 1
 LEVELS = 2 * S_STEP
-MESH = pl.DeviceIdType.MESH
+LOGICAL = pl.DeviceIdType.LOGICAL
 HIGHEST = lax.Precision.HIGHEST
 
 
@@ -57,23 +57,21 @@
     member = within * ngrp + grp
     sub_up, sub_down = lax.rem(sub + 1, nsub), lax.rem(sub + nsub - 1, nsub)
     grp_up, grp_down = lax.rem(grp + 1, ngrp), lax.rem(grp + ngrp - 1, ngrp)
-    next_sub, prev_sub = (sub_up, grp), (sub_down, grp)
-    next_grp, prev_grp = (sub, grp_up), (sub, grp_down)
-
-    def any_peer(offset):
-        other = lax.rem(me + offset, devices)
-        return (lax.div(other, ngrp), lax.rem(other, ngrp))
+    next_sub, prev_sub = sub_up * ngrp + grp, sub_down * ngrp + grp
+    next_grp, prev_grp = sub * ngrp + grp_up, sub * ngrp + grp_down
+    diagonal_peers = (sub_up * ngrp + grp_down, sub_down * ngrp + grp_up)
 
     def to_all(action):
         def step(offset, carry):
-            action(any_peer(offset))
+            other = me + offset
+            action(jnp.where(other >= devices, other - devices, other))
             return carry
 
         lax.fori_loop(1, devices, step, 0)
 
     near_others = [lax.rem(member + o, members) for o in range(1, members)]
-    near_peers = [(plane * inner + lax.div(o, ngrp), lax.rem(o, ngrp)) for o in near_others]
-    far_peers = [(lax.rem(plane + o, planes) * inner + within, grp) for o in range(1, planes)]
+    near_peers = [plane * members + o for o in near_others]
+    far_peers = [lax.rem(plane + o, planes) * members + member for o in range(1, planes)]
 
     barrier = pltpu.get_barrier_semaphore()
     loads = [
@@ -89,12 +87,12 @@
     ]
     for copy in loads:
         copy.start()
-    to_all(lambda peer: pl.semaphore_signal(barrier, inc=1, device_id=peer, device_id_type=MESH))
+    to_all(lambda peer: pl.semaphore_signal(barrier, inc=1, device_id=peer, device_id_type=LOGICAL))
 
     def send(src, dst, send_sem, recv_sem, peer):
         copy = pltpu.make_async_remote_copy(
             src_ref=src, dst_ref=dst, send_sem=send_sem, recv_sem=recv_sem,
-            device_id=peer, device_id_type=MESH,
+            device_id=peer, device_id_type=LOGICAL,
         )
         copy.start()
         return copy
@@ -106,7 +104,7 @@
         part = buf.at[pl.ds(0, count - 1)]
         copy = pltpu.make_async_remote_copy(
             src_ref=part, dst_ref=part, send_sem=send_sem, recv_sem=recv_sem,
-            device_id=peer, device_id_type=MESH,
+            device_id=peer, device_id_type=LOGICAL,
         )
         copy.wait_recv()
         pending.append(copy)
@@ -200,13 +198,15 @@
         ]
         diags = [
             send(up_out.at[level, d], diag_in.at[level, d], diag_send.at[level, d], diag_recv.at[level, d], peer)
-            for d, peer in enumerate(((sub_up, grp_down), (sub_down, grp_up)))
-        ]
+            for d, peer in enumerate(diagonal_peers)
+        ] if level > 0 else []
         pending += ups + diags
-        if level == 0:
+        if level > 0:
+            part = coarse_part(packed)
+        else:
+            own = rows_c.at[me]
+            to_all(lambda peer: send(own, own, rows_send, rows_recv, peer))
             loads[5].wait()
-        else:
-            part = coarse_part(packed)
 
         def own_part(first):
             columns = slice(first, first + face)
@@ -215,29 +215,27 @@
         def low_part(value, first, column):
             return dot(value, inv[first : first + face, column : column + face])
 
-        low_out[level, 0] = own_part(face)
-        low_out[level, 1] = own_part(3 * face)
-        lows = [
-            send(low_out.at[level, d], low_in.at[level, d], low_send.at[level, d], low_recv.at[level, d], peer)
-            for d, peer in enumerate((prev_sub, prev_grp))
-        ]
-        pending += lows
-        if level == 0:
-            own = rows_c.at[me]
-            to_all(lambda peer: send(own, own, rows_send, rows_recv, peer))
-            blocks = [
-                send(
-                    inv.at[pl.ds(first, face), pl.ds(column, face)], landing.at[d],
-                    edge_send.at[i], edge_recv.at[i], peer,
-                )
-                for i, (first, column, landing, d, peer) in enumerate((
-                    (face, face, edge, 0, prev_sub),
-                    (3 * face, 3 * face, edge, 1, prev_grp),
-                    (3 * face, face, cross, 0, prev_sub),
-                    (face, 3 * face, cross, 1, prev_grp),
-                ))
+        def send_lows(first, second):
+            low_out[level, 0] = first.astype(low_out.dtype)
+            low_out[level, 1] = second.astype(low_out.dtype)
+            copies = [
+                send(low_out.at[level, d], low_in.at[level, d], low_send.at[level, d], low_recv.at[level, d], peer)
+                for d, peer in enumerate((prev_sub, prev_grp))
             ]
-            pending += blocks
+            pending.extend(copies)
+            return copies
+
+        first_low, second_low = own_part(face), own_part(3 * face)
+        if level > 0:
+            lows = send_lows(first_low, second_low)
+        else:
+            for copy in ups:
+                copy.wait_recv()
+            low_sub, low_grp = up_in[level, 0], up_in[level, 1]
+            lows = send_lows(
+                first_low - low_part(low_sub, face, face) - low_part(low_grp, 3 * face, face),
+                second_low - low_part(low_sub, face, 3 * face) - low_part(low_grp, 3 * face, 3 * face),
+            )
             for copy in term_copies:
                 copy.wait_recv()
             weight = jnp.concatenate(
@@ -248,6 +246,20 @@
             load_rest[...] = jnp.concatenate([weight_rest] * pack, axis=0)
             part = coarse_part(packed)
         send_coarse(level, part)
+        if level == 0:
+            blocks = [
+                send(
+                    inv.at[pl.ds(first, face), pl.ds(column, face)], landing.at[d],
+                    edge_send.at[i], edge_recv.at[i], peer,
+                )
+                for i, (first, column, landing, d, peer) in enumerate((
+                    (face, face, edge, 0, prev_sub),
+                    (3 * face, face, cross, 0, prev_sub),
+                    (3 * face, 3 * face, edge, 1, prev_grp),
+                    (face, 3 * face, cross, 1, prev_grp),
+                ))
+            ]
+            pending += blocks
         packed, remainder = keep(level, x)
         if level == LEVELS - 1:
             count = LEVELS * right
@@ -259,9 +271,10 @@
                 send(part_out.at[other], part_near.at[member], part_send.at[0], part_recv.at[0], peer)
         up_sub = own_part(0)
         up_grp = own_part(2 * face)
-        for copy in ups:
-            copy.wait_recv()
-        low_sub, low_grp = up_in[level, 0], up_in[level, 1]
+        if level > 0:
+            for copy in ups:
+                copy.wait_recv()
+            low_sub, low_grp = up_in[level, 0], up_in[level, 1]
         up_sub = up_sub - low_part(low_sub, face, 0) - low_part(low_grp, 3 * face, 0)
         up_grp = up_grp - low_part(low_sub, face, 2 * face) - low_part(low_grp, 3 * face, 2 * face)
         if level == 0:
@@ -270,18 +283,20 @@
             raised_high, raised_rest = split(raised)
             lift_high[...] = jnp.concatenate([raised_high] * pack, axis=0)
             lift_rest[...] = jnp.concatenate([raised_rest] * pack, axis=0)
-            for copy in blocks:
+        else:
+            if level == 1:
+                for copy in blocks:
+                    copy.wait_recv()
+            up_sub = up_sub + dot(x_sub, edge[0])
+            up_grp = up_grp + dot(x_grp, edge[1])
+            for copy in diags:
                 copy.wait_recv()
-        up_sub = up_sub + dot(x_sub, edge[0])
-        up_grp = up_grp + dot(x_grp, edge[1])
-        for copy in diags:
-            copy.wait_recv()
-        up_sub = up_sub + dot(diag_in[level, 1], cross[0])
-        up_grp = up_grp + dot(diag_in[level, 0], cross[1])
+            up_sub = up_sub + dot(diag_in[level, 1], cross[0])
+            up_grp = up_grp + dot(diag_in[level, 0], cross[1])
         base = jnp.concatenate([up_sub, up_grp], axis=1) - centre * x
         for copy in lows:
             copy.wait_recv()
-        base = base - jnp.concatenate([low_in[level, 0], low_in[level, 1]], axis=1)
+        base = base - jnp.concatenate([low_in[level, 0], low_in[level, 1]], axis=1).astype(jnp.float32)
         landed(direct.at[level], devices, direct_send.at[level], direct_recv.at[level], next_grp)
         image = base + coarse_lift(added(direct.at[level], devices))
         following = image * scale if level == 0 else 2.0 * image * scale - previous
@@ -353,8 +368,8 @@
             pltpu.VMEM((LEVELS, 2, right, face), bf16),
             pltpu.VMEM((LEVELS, 2, right, face), bf16),
             pltpu.VMEM((LEVELS, 2, right, face), bf16),
-            pltpu.VMEM((LEVELS, 2, right, face), f32),
-            pltpu.VMEM((LEVELS, 2, right, face), f32),
+            pltpu.VMEM((LEVELS, 2, right, face), bf16),
+            pltpu.VMEM((LEVELS, 2, right, face), bf16),
             pltpu.VMEM((2, nco, face), f32),
             pltpu.VMEM((2, nco, face), f32),
             pltpu.VMEM((2, face, face), bf16),

time: 47 us -> 48.8 us (1.038)
  Pallas kernels: 43.1 us -> 44.9 us
    pallas_call x1, Pallas kernels: 43.1 us -> 44.9 us  [body(): pl.pallas_call(functools.partial(kernel, nsub, ngrp, inner, pack), out_sh...]
where the time goes in v4:
time: 48.8 us; the launch traced here: 48.6 us
  Pallas kernels  44.9 us (92%)
  local copies, waits for them, and re-layouts  2.99 us (6%)
  between operations  0.64 us (1%)
    pallas_call x1, Pallas kernels, body(): pl.pallas_call(functools.partial(kernel, nsub, ngrp, inner, pack), out_sh...  44.9 us
    unnamed x2, local copies, waits for them, and re-layouts  2.99 us

profile of v4, /device:TPU:0, one launch (start us, length us, event | category | flops | bytes accessed | tf_op | source)
XLA Modules:
  0.0 48.6 jit_solution(12790336256169060805)
XLA Ops:
  0.6 44.9 %shard_map.77 = (f32[5,16,1,1,512]{4,3,2,1,0:T(1,128)}, f32[80,80]{1,0:T(8,128)}) custom-call(f32[2]{0:T(128)} %bounds_hbm.1, f32[16,1,1,512]{3,2,1,0:T(1,128)} %res_hbm.1, bf16[1,1,1024,1024]{3,2,1,0:T(8,128)(2,1)} %inv_hbm.1, bf16[1,1,24,1024]{3,2,1,0:T(8,128)(2,1)} %corner_hbm.1, s32[1,1,24]{2,1,0:T(1,128)} %map_hbm.1, f32[1,32]{1,0:T(1,128)} %coarse_hbm.1), custom_call_target="tpu_custom_call" | custom-call | tf_op jit(solution)/shard_map/pallas_call | solution.py:352
  45.6 1.6 %copy.10 = f32[5,16,1,1,512]{4,3,2,1,0:T(1,128)} copy(f32[5,16,1,1,512]{4,3,2,1,0:T(1,128)} %get-tuple-element.4) | data formatting | bytes 327680
  47.2 1.4 %copy.11 = f32[80,80]{1,0:T(8,128)} copy(f32[80,80]{1,0:T(8,128)} %get-tuple-element.5) | data formatting | bytes 51200

commit v5 on v3

--- a/solution.py
+++ b/solution.py
@@ -10,7 +10,7 @@
 S_STEP = 2
 BLOCKS = 2 * S_STEP + 1
 LEVELS = 2 * S_STEP
-MESH = pl.DeviceIdType.MESH
+LOGICAL = pl.DeviceIdType.LOGICAL
 HIGHEST = lax.Precision.HIGHEST
 
 
@@ -57,23 +57,21 @@
     member = within * ngrp + grp
     sub_up, sub_down = lax.rem(sub + 1, nsub), lax.rem(sub + nsub - 1, nsub)
     grp_up, grp_down = lax.rem(grp + 1, ngrp), lax.rem(grp + ngrp - 1, ngrp)
-    next_sub, prev_sub = (sub_up, grp), (sub_down, grp)
-    next_grp, prev_grp = (sub, grp_up), (sub, grp_down)
-
-    def any_peer(offset):
-        other = lax.rem(me + offset, devices)
-        return (lax.div(other, ngrp), lax.rem(other, ngrp))
+    next_sub, prev_sub = sub_up * ngrp + grp, sub_down * ngrp + grp
+    next_grp, prev_grp = sub * ngrp + grp_up, sub * ngrp + grp_down
+    diagonal_peers = (sub_up * ngrp + grp_down, sub_down * ngrp + grp_up)
 
     def to_all(action):
         def step(offset, carry):
-            action(any_peer(offset))
+            other = me + offset
+            action(jnp.where(other >= devices, other - devices, other))
             return carry
 
-        lax.fori_loop(1, devices, step, 0)
+        lax.fori_loop(1, devices, step, 0, unroll=devices <= 64)
 
     near_others = [lax.rem(member + o, members) for o in range(1, members)]
-    near_peers = [(plane * inner + lax.div(o, ngrp), lax.rem(o, ngrp)) for o in near_others]
-    far_peers = [(lax.rem(plane + o, planes) * inner + within, grp) for o in range(1, planes)]
+    near_peers = [plane * members + o for o in near_others]
+    far_peers = [lax.rem(plane + o, planes) * members + member for o in range(1, planes)]
 
     barrier = pltpu.get_barrier_semaphore()
     loads = [
@@ -89,12 +87,12 @@
     ]
     for copy in loads:
         copy.start()
-    to_all(lambda peer: pl.semaphore_signal(barrier, inc=1, device_id=peer, device_id_type=MESH))
+    to_all(lambda peer: pl.semaphore_signal(barrier, inc=1, device_id=peer, device_id_type=LOGICAL))
 
     def send(src, dst, send_sem, recv_sem, peer):
         copy = pltpu.make_async_remote_copy(
             src_ref=src, dst_ref=dst, send_sem=send_sem, recv_sem=recv_sem,
-            device_id=peer, device_id_type=MESH,
+            device_id=peer, device_id_type=LOGICAL,
         )
         copy.start()
         return copy
@@ -106,7 +104,7 @@
         part = buf.at[pl.ds(0, count - 1)]
         copy = pltpu.make_async_remote_copy(
             src_ref=part, dst_ref=part, send_sem=send_sem, recv_sem=recv_sem,
-            device_id=peer, device_id_type=MESH,
+            device_id=peer, device_id_type=LOGICAL,
         )
         copy.wait_recv()
         pending.append(copy)
@@ -200,7 +198,7 @@
         ]
         diags = [
             send(up_out.at[level, d], diag_in.at[level, d], diag_send.at[level, d], diag_recv.at[level, d], peer)
-            for d, peer in enumerate(((sub_up, grp_down), (sub_down, grp_up)))
+            for d, peer in enumerate(diagonal_peers)
         ]
         pending += ups + diags
         if level == 0:
@@ -223,8 +221,6 @@
         ]
         pending += lows
         if level == 0:
-            own = rows_c.at[me]
-            to_all(lambda peer: send(own, own, rows_send, rows_recv, peer))
             blocks = [
                 send(
                     inv.at[pl.ds(first, face), pl.ds(column, face)], landing.at[d],
@@ -238,6 +234,8 @@
                 ))
             ]
             pending += blocks
+            own = rows_c.at[me]
+            to_all(lambda peer: send(own, own, rows_send, rows_recv, peer))
             for copy in term_copies:
                 copy.wait_recv()
             weight = jnp.concatenate(

time: 47 us -> 46.9 us (level)
  no operation moved by 1% of the time
where the time goes in v5:
time: 46.9 us; the launch traced here: 46.7 us
  Pallas kernels  43.1 us (92%)
  local copies, waits for them, and re-layouts  2.99 us (6%)
  between operations  0.64 us (1%)
    pallas_call x1, Pallas kernels, body(): pl.pallas_call(functools.partial(kernel, nsub, ngrp, inner, pack), out_sh...  43.1 us
    unnamed x2, local copies, waits for them, and re-layouts  2.99 us

profile of v5, /device:TPU:0, one launch (start us, length us, event | category | flops | bytes accessed | tf_op | source)
XLA Modules:
  0.0 46.7 jit_solution(3651292705698960518)
XLA Ops:
  0.6 43.1 %shard_map.77 = (f32[5,16,1,1,512]{4,3,2,1,0:T(1,128)}, f32[80,80]{1,0:T(8,128)}) custom-call(f32[2]{0:T(128)} %bounds_hbm.1, f32[16,1,1,512]{3,2,1,0:T(1,128)} %res_hbm.1, bf16[1,1,1024,1024]{3,2,1,0:T(8,128)(2,1)} %inv_hbm.1, bf16[1,1,24,1024]{3,2,1,0:T(8,128)(2,1)} %corner_hbm.1, s32[1,1,24]{2,1,0:T(1,128)} %map_hbm.1, f32[1,32]{1,0:T(1,128)} %coarse_hbm.1), custom_call_target="tpu_custom_call" | custom-call | tf_op jit(solution)/shard_map/pallas_call | solution.py:335
  43.7 1.6 %copy.10 = f32[5,16,1,1,512]{4,3,2,1,0:T(1,128)} copy(f32[5,16,1,1,512]{4,3,2,1,0:T(1,128)} %get-tuple-element.4) | data formatting | bytes 327680
  45.3 1.4 %copy.11 = f32[80,80]{1,0:T(8,128)} copy(f32[80,80]{1,0:T(8,128)} %get-tuple-element.5) | data formatting | bytes 51200

commit v6 on v4

--- a/solution.py
+++ b/solution.py
@@ -67,7 +67,7 @@
             action(jnp.where(other >= devices, other - devices, other))
             return carry
 
-        lax.fori_loop(1, devices, step, 0)
+        lax.fori_loop(1, devices, step, 0, unroll=devices <= 64)
 
     near_others = [lax.rem(member + o, members) for o in range(1, members)]
     near_peers = [plane * members + o for o in near_others]
@@ -204,9 +204,22 @@
         if level > 0:
             part = coarse_part(packed)
         else:
+            loads[5].wait()
+            blocks = [
+                send(
+                    inv.at[pl.ds(first, face), pl.ds(column, face)], landing.at[d],
+                    edge_send.at[i], edge_recv.at[i], peer,
+                )
+                for i, (first, column, landing, d, peer) in enumerate((
+                    (face, face, edge, 0, prev_sub),
+                    (3 * face, face, cross, 0, prev_sub),
+                    (3 * face, 3 * face, edge, 1, prev_grp),
+                    (face, 3 * face, cross, 1, prev_grp),
+                ))
+            ]
+            pending += blocks
             own = rows_c.at[me]
             to_all(lambda peer: send(own, own, rows_send, rows_recv, peer))
-            loads[5].wait()
 
         def own_part(first):
             columns = slice(first, first + face)
@@ -216,8 +229,8 @@
             return dot(value, inv[first : first + face, column : column + face])
 
         def send_lows(first, second):
-            low_out[level, 0] = first.astype(low_out.dtype)
-            low_out[level, 1] = second.astype(low_out.dtype)
+            low_out[level, 0] = first
+            low_out[level, 1] = second
             copies = [
                 send(low_out.at[level, d], low_in.at[level, d], low_send.at[level, d], low_recv.at[level, d], peer)
                 for d, peer in enumerate((prev_sub, prev_grp))
@@ -246,20 +259,6 @@
             load_rest[...] = jnp.concatenate([weight_rest] * pack, axis=0)
             part = coarse_part(packed)
         send_coarse(level, part)
-        if level == 0:
-            blocks = [
-                send(
-                    inv.at[pl.ds(first, face), pl.ds(column, face)], landing.at[d],
-                    edge_send.at[i], edge_recv.at[i], peer,
-                )
-                for i, (first, column, landing, d, peer) in enumerate((
-                    (face, face, edge, 0, prev_sub),
-                    (3 * face, face, cross, 0, prev_sub),
-                    (3 * face, 3 * face, edge, 1, prev_grp),
-                    (face, 3 * face, cross, 1, prev_grp),
-                ))
-            ]
-            pending += blocks
         packed, remainder = keep(level, x)
         if level == LEVELS - 1:
             count = LEVELS * right
@@ -296,7 +295,7 @@
         base = jnp.concatenate([up_sub, up_grp], axis=1) - centre * x
         for copy in lows:
             copy.wait_recv()
-        base = base - jnp.concatenate([low_in[level, 0], low_in[level, 1]], axis=1).astype(jnp.float32)
+        base = base - jnp.concatenate([low_in[level, 0], low_in[level, 1]], axis=1)
         landed(direct.at[level], devices, direct_send.at[level], direct_recv.at[level], next_grp)
         image = base + coarse_lift(added(direct.at[level], devices))
         following = image * scale if level == 0 else 2.0 * image * scale - previous
@@ -368,8 +367,8 @@
             pltpu.VMEM((LEVELS, 2, right, face), bf16),
             pltpu.VMEM((LEVELS, 2, right, face), bf16),
             pltpu.VMEM((LEVELS, 2, right, face), bf16),
-            pltpu.VMEM((LEVELS, 2, right, face), bf16),
-            pltpu.VMEM((LEVELS, 2, right, face), bf16),
+            pltpu.VMEM((LEVELS, 2, right, face), f32),
+            pltpu.VMEM((LEVELS, 2, right, face), f32),
             pltpu.VMEM((2, nco, face), f32),
             pltpu.VMEM((2, nco, face), f32),
             pltpu.VMEM((2, face, face), bf16),

time: 48.8 us -> 48.6 us (level)
  no operation moved by 1% of the time
where the time goes in v6:
time: 48.6 us; the launch traced here: 48.4 us
  Pallas kernels  44.8 us (92%)
  local copies, waits for them, and re-layouts  2.99 us (6%)
  between operations  0.64 us (1%)
    pallas_call x1, Pallas kernels, body(): pl.pallas_call(functools.partial(kernel, nsub, ngrp, inner, pack), out_sh...  44.8 us
    unnamed x2, local copies, waits for them, and re-layouts  2.99 us

profile of v6, /device:TPU:0, one launch (start us, length us, event | category | flops | bytes accessed | tf_op | source)
XLA Modules:
  0.0 48.4 jit_solution(16287929883282334505)
XLA Ops:
  0.6 44.8 %shard_map.77 = (f32[5,16,1,1,512]{4,3,2,1,0:T(1,128)}, f32[80,80]{1,0:T(8,128)}) custom-call(f32[2]{0:T(128)} %bounds_hbm.1, f32[16,1,1,512]{3,2,1,0:T(1,128)} %res_hbm.1, bf16[1,1,1024,1024]{3,2,1,0:T(8,128)(2,1)} %inv_hbm.1, bf16[1,1,24,1024]{3,2,1,0:T(8,128)(2,1)} %corner_hbm.1, s32[1,1,24]{2,1,0:T(1,128)} %map_hbm.1, f32[1,32]{1,0:T(1,128)} %coarse_hbm.1), custom_call_target="tpu_custom_call" | custom-call | tf_op jit(solution)/shard_map/pallas_call | solution.py:351
  45.4 1.6 %copy.10 = f32[5,16,1,1,512]{4,3,2,1,0:T(1,128)} copy(f32[5,16,1,1,512]{4,3,2,1,0:T(1,128)} %get-tuple-element.4) | data formatting | bytes 327680
  47.0 1.4 %copy.11 = f32[80,80]{1,0:T(8,128)} copy(f32[80,80]{1,0:T(8,128)} %get-tuple-element.5) | data formatting | bytes 51200

commit v7 on v6

--- a/solution.py
+++ b/solution.py
@@ -124,6 +124,17 @@
         for peer in peers:
             send(own, own, send_sem, recv_sem, peer)
 
+    def send_blocks(place, landing, corners_of):
+        copies = [
+            send(
+                inv.at[pl.ds(first, face), pl.ds(column, face)], landing.at[d],
+                edge_send.at[place + d], edge_recv.at[place + d], peer,
+            )
+            for d, ((first, column), peer) in enumerate(zip(corners_of, (prev_sub, prev_grp)))
+        ]
+        pending.extend(copies)
+        return copies
+
     high[...] = jnp.zeros_like(high)
     rest[...] = jnp.zeros_like(rest)
     loads[0].wait()
@@ -204,22 +215,10 @@
         if level > 0:
             part = coarse_part(packed)
         else:
-            loads[5].wait()
-            blocks = [
-                send(
-                    inv.at[pl.ds(first, face), pl.ds(column, face)], landing.at[d],
-                    edge_send.at[i], edge_recv.at[i], peer,
-                )
-                for i, (first, column, landing, d, peer) in enumerate((
-                    (face, face, edge, 0, prev_sub),
-                    (3 * face, face, cross, 0, prev_sub),
-                    (3 * face, 3 * face, edge, 1, prev_grp),
-                    (face, 3 * face, cross, 1, prev_grp),
-                ))
-            ]
-            pending += blocks
             own = rows_c.at[me]
             to_all(lambda peer: send(own, own, rows_send, rows_recv, peer))
+            loads[5].wait()
+            blocks = send_blocks(0, edge, ((face, face), (3 * face, 3 * face)))
 
         def own_part(first):
             columns = slice(first, first + face)
@@ -242,13 +241,6 @@
         if level > 0:
             lows = send_lows(first_low, second_low)
         else:
-            for copy in ups:
-                copy.wait_recv()
-            low_sub, low_grp = up_in[level, 0], up_in[level, 1]
-            lows = send_lows(
-                first_low - low_part(low_sub, face, face) - low_part(low_grp, 3 * face, face),
-                second_low - low_part(low_sub, face, 3 * face) - low_part(low_grp, 3 * face, 3 * face),
-            )
             for copy in term_copies:
                 copy.wait_recv()
             weight = jnp.concatenate(
@@ -259,6 +251,15 @@
             load_rest[...] = jnp.concatenate([weight_rest] * pack, axis=0)
             part = coarse_part(packed)
         send_coarse(level, part)
+        if level == 0:
+            for copy in ups:
+                copy.wait_recv()
+            low_sub, low_grp = up_in[level, 0], up_in[level, 1]
+            lows = send_lows(
+                first_low - low_part(low_sub, face, face) - low_part(low_grp, 3 * face, face),
+                second_low - low_part(low_sub, face, 3 * face) - low_part(low_grp, 3 * face, 3 * face),
+            )
+            blocks += send_blocks(2, cross, ((3 * face, face), (face, 3 * face)))
         packed, remainder = keep(level, x)
         if level == LEVELS - 1:
             count = LEVELS * right

time: 48.6 us -> 46.8 us (0.963)
  Pallas kernels: 44.8 us -> 42.9 us
    pallas_call x1, Pallas kernels: 44.8 us -> 42.9 us  [body(): pl.pallas_call(functools.partial(kernel, nsub, ngrp, inner, pack), out_sh...]
where the time goes in v7:
time: 46.8 us; the launch traced here: 46.5 us
  Pallas kernels  42.9 us (92%)
  local copies, waits for them, and re-layouts  2.99 us (6%)
  between operations  0.64 us (1%)
    pallas_call x1, Pallas kernels, body(): pl.pallas_call(functools.partial(kernel, nsub, ngrp, inner, pack), out_sh...  42.9 us
    unnamed x2, local copies, waits for them, and re-layouts  2.99 us

profile of v7, /device:TPU:0, one launch (start us, length us, event | category | flops | bytes accessed | tf_op | source)
XLA Modules:
  0.0 46.5 jit_solution(9064038171246042898)
XLA Ops:
  0.6 42.9 %shard_map.77 = (f32[5,16,1,1,512]{4,3,2,1,0:T(1,128)}, f32[80,80]{1,0:T(8,128)}) custom-call(f32[2]{0:T(128)} %bounds_hbm.1, f32[16,1,1,512]{3,2,1,0:T(1,128)} %res_hbm.1, bf16[1,1,1024,1024]{3,2,1,0:T(8,128)(2,1)} %inv_hbm.1, bf16[1,1,24,1024]{3,2,1,0:T(8,128)(2,1)} %corner_hbm.1, s32[1,1,24]{2,1,0:T(1,128)} %map_hbm.1, f32[1,32]{1,0:T(1,128)} %coarse_hbm.1), custom_call_target="tpu_custom_call" | custom-call | tf_op jit(solution)/shard_map/pallas_call | solution.py:352
  43.5 1.6 %copy.10 = f32[5,16,1,1,512]{4,3,2,1,0:T(1,128)} copy(f32[5,16,1,1,512]{4,3,2,1,0:T(1,128)} %get-tuple-element.4) | data formatting | bytes 327680
  45.1 1.4 %copy.11 = f32[80,80]{1,0:T(8,128)} copy(f32[80,80]{1,0:T(8,128)} %get-tuple-element.5) | data formatting | bytes 51200

commit v8 on v7

--- a/solution.py
+++ b/solution.py
@@ -85,9 +85,12 @@
             (inv_hbm.at[0, 0], inv),
         ))
     ]
-    for copy in loads:
+    for copy in loads[:3]:
         copy.start()
     to_all(lambda peer: pl.semaphore_signal(barrier, inc=1, device_id=peer, device_id_type=LOGICAL))
+
+    for copy in loads[3:]:
+        copy.start()
 
     def send(src, dst, send_sem, recv_sem, peer):
         copy = pltpu.make_async_remote_copy(
@@ -331,6 +334,17 @@
         copy.wait()
 
 
+def hand_over(basis_from, gram_from, basis_to, gram_to, sems):
+    copies = [
+        pltpu.make_async_copy(basis_from, basis_to, sems.at[0]),
+        pltpu.make_async_copy(gram_from, gram_to, sems.at[1]),
+    ]
+    for copy in copies:
+        copy.start()
+    for copy in copies:
+        copy.wait()
+
+
 def body(nsub, ngrp, residual, bounds, local_inverse, corner_basis, corner_map, coarse_inverse):
     right, half = residual.shape[0], residual.shape[3]
     face = half // 2
@@ -349,12 +363,14 @@
     hbm = pl.BlockSpec(memory_space=pltpu.HBM)
     dma = pltpu.SemaphoreType.DMA
     f32, bf16 = jnp.float32, jnp.bfloat16
-    return pl.pallas_call(
+    shapes = (
+        jax.ShapeDtypeStruct((BLOCKS, right, 1, 1, half), f32),
+        jax.ShapeDtypeStruct((order, order), f32),
+    )
+    limit = 60 * 1024 * 1024
+    results = pl.pallas_call(
         functools.partial(kernel, nsub, ngrp, inner, pack),
-        out_shape=(
-            jax.ShapeDtypeStruct((BLOCKS, right, 1, 1, half), f32),
-            jax.ShapeDtypeStruct((order, order), f32),
-        ),
+        out_shape=shapes,
         in_specs=[hbm] * 6,
         out_specs=(hbm, hbm),
         scratch_shapes=[
@@ -412,9 +428,17 @@
             dma,
         ],
         compiler_params=pltpu.CompilerParams(
-            collective_id=0, has_side_effects=True, vmem_limit_bytes=60 * 1024 * 1024
+            collective_id=0, has_side_effects=True, vmem_limit_bytes=limit
         ),
     )(bounds, residual, local_inverse, corner_basis, corner_map, coarse_inverse)
+    return pl.pallas_call(
+        hand_over,
+        out_shape=shapes,
+        in_specs=[hbm, hbm],
+        out_specs=(hbm, hbm),
+        scratch_shapes=[dma((2,))],
+        compiler_params=pltpu.CompilerParams(vmem_limit_bytes=limit),
+    )(*results)
 
 
 def solution(mesh):

time: 46.8 us -> 51 us (1.090)
  Pallas kernels: 42.9 us -> 50.2 us
  local copies, waits for them, and re-layouts: 2.99 us -> 0 us
    pallas_call x0 -> x1, Pallas kernels: none -> 7.32 us  [body(): pl.pallas_call(hand_over, out_shape=shapes, in_specs=[hbm, hbm], out_spec...]
    unnamed x2 -> x0, local copies, waits for them, and re-layouts: 2.99 us -> none
where the time goes in v8:
time: 51 us; the launch traced here: 50.9 us
  Pallas kernels  50.2 us (98%)
  between operations  0.64 us (1%)
    pallas_call x1, Pallas kernels, body(): pl.pallas_call(functools.partial(kernel, nsub, ngrp, inner, pack), out_sh...  42.9 us
    pallas_call x1, Pallas kernels, body(): pl.pallas_call(hand_over, out_shape=shapes, in_specs=[hbm, hbm], out_spec...  7.32 us

profile of v8, /device:TPU:0, one launch (start us, length us, event | category | flops | bytes accessed | tf_op | source)
XLA Modules:
  0.0 50.9 jit_solution(2699536091490063401)
XLA Ops:
  0.6 42.9 %shard_map.77 = (f32[5,16,1,1,512]{4,3,2,1,0:T(1,128)}, f32[80,80]{1,0:T(8,128)}) custom-call(f32[2]{0:T(128)} %bounds_hbm.1, f32[16,1,1,512]{3,2,1,0:T(1,128)} %res_hbm.1, bf16[1,1,1024,1024]{3,2,1,0:T(8,128)(2,1)} %inv_hbm.1, bf16[1,1,24,1024]{3,2,1,0:T(8,128)(2,1)} %corner_hbm.1, s32[1,1,24]{2,1,0:T(1,128)} %map_hbm.1, f32[1,32]{1,0:T(1,128)} %coarse_hbm.1), custom_call_target="tpu_custom_call" | custom-call | tf_op jit(solution)/shard_map/pallas_call | solution.py:371
  43.5 7.3 %shard_map.78 = (f32[5,16,1,1,512]{4,3,2,1,0:T(1,128)}, f32[80,80]{1,0:T(8,128)}) custom-call(f32[5,16,1,1,512]{4,3,2,1,0:T(1,128)} %get-tuple-element.4.basis_from, f32[80,80]{1,0:T(8,128)} %get-tuple-element.5.gram_from), custom_call_target="tpu_custom_call" | custom-call | tf_op jit(solution)/shard_map/pallas_call | solution.py:434

commit v9 on v7

--- a/solution.py
+++ b/solution.py
@@ -85,9 +85,12 @@
             (inv_hbm.at[0, 0], inv),
         ))
     ]
-    for copy in loads:
+    for copy in loads[:3]:
         copy.start()
     to_all(lambda peer: pl.semaphore_signal(barrier, inc=1, device_id=peer, device_id_type=LOGICAL))
+
+    for copy in loads[3:]:
+        copy.start()
 
     def send(src, dst, send_sem, recv_sem, peer):
         copy = pltpu.make_async_remote_copy(
@@ -183,7 +186,7 @@
 
     def keep(level, value):
         packed, remainder = split(value)
-        basis_ref[level, :, 0, 0, :] = value
+        basis_ref[level] = value
         high[pl.ds(level * right, right), :] = packed
         rest[pl.ds(level * right, right), :] = remainder
         stores.append(pltpu.make_async_copy(basis_ref.at[level], basis_hbm.at[level], store_sem.at[level]))
@@ -322,7 +325,7 @@
     column = lax.broadcasted_iota(jnp.int32, (order, order), 1)
     below = jnp.where(lax.div(column, right) < lax.div(row, right), full, 0.0)
     same = jnp.where(lax.div(column, right) == lax.div(row, right), full, 0.0)
-    gram_ref[...] = (below + same + below.T) * (1.0 / (half * nsub))
+    gram_ref[...] = below + same + below.T
     stores.append(pltpu.make_async_copy(gram_ref, gram_hbm, store_sem.at[BLOCKS]))
     stores[-1].start()
     for copy in pending:
@@ -349,16 +352,16 @@
     hbm = pl.BlockSpec(memory_space=pltpu.HBM)
     dma = pltpu.SemaphoreType.DMA
     f32, bf16 = jnp.float32, jnp.bfloat16
-    return pl.pallas_call(
+    basis, gram = pl.pallas_call(
         functools.partial(kernel, nsub, ngrp, inner, pack),
         out_shape=(
-            jax.ShapeDtypeStruct((BLOCKS, right, 1, 1, half), f32),
+            jax.ShapeDtypeStruct((BLOCKS, right, half), f32),
             jax.ShapeDtypeStruct((order, order), f32),
         ),
         in_specs=[hbm] * 6,
         out_specs=(hbm, hbm),
         scratch_shapes=[
-            pltpu.VMEM((BLOCKS, right, 1, 1, half), f32),
+            pltpu.VMEM((BLOCKS, right, half), f32),
             pltpu.VMEM((order, order), f32),
             pltpu.SMEM(bounds.shape, f32),
             pltpu.VMEM(residual.shape, f32),
@@ -415,6 +418,7 @@
             collective_id=0, has_side_effects=True, vmem_limit_bytes=60 * 1024 * 1024
         ),
     )(bounds, residual, local_inverse, corner_basis, corner_map, coarse_inverse)
+    return basis.reshape(BLOCKS, right, 1, 1, half), gram * (1.0 / (half * nsub))
 
 
 def solution(mesh):

time: 46.8 us -> 46.9 us (level)
  other arithmetic: 0 us -> 1.4 us
  local copies, waits for them, and re-layouts: 2.99 us -> 1.75 us
    mul x0 -> x1, other arithmetic: none -> 1.4 us  [body(): gram * (1.0 / (half * nsub))]
    unnamed x2 -> x1, local copies, waits for them, and re-layouts: 2.99 us -> 1.75 us
where the time goes in v9:
time: 46.9 us; the launch traced here: 46.7 us
  Pallas kernels  42.9 us (91%)
  local copies, waits for them, and re-layouts  1.75 us (4%)
  other arithmetic  1.4 us (3%)
  between operations  0.64 us (1%)
    pallas_call x1, Pallas kernels, body(): pl.pallas_call(functools.partial(kernel, nsub, ngrp, inner, pack), out_sh...  42.9 us
    unnamed x1, local copies, waits for them, and re-layouts  1.75 us
    mul x1, other arithmetic, body(): gram * (1.0 / (half * nsub))  1.4 us

profile of v9, /device:TPU:0, one launch (start us, length us, event | category | flops | bytes accessed | tf_op | source)
XLA Modules:
  0.0 46.7 jit_solution(16858791186434402949)
XLA Ops:
  0.6 42.9 %shard_map.77 = (f32[5,16,512]{2,1,0:T(8,128)}, f32[80,80]{1,0:T(8,128)}) custom-call(f32[2]{0:T(128)} %bounds_hbm.1, f32[16,1,1,512]{3,2,1,0:T(1,128)} %res_hbm.1, bf16[1,1,1024,1024]{3,2,1,0:T(8,128)(2,1)} %inv_hbm.1, bf16[1,1,24,1024]{3,2,1,0:T(8,128)(2,1)} %corner_hbm.1, s32[1,1,24]{2,1,0:T(1,128)} %map_hbm.1, f32[1,32]{1,0:T(1,128)} %coarse_hbm.1), custom_call_target="tpu_custom_call" | custom-call | tf_op jit(solution)/shard_map/pallas_call | solution.py:355
  43.5 1.8 %copy.8 = f32[5,16,1,1,512]{4,3,2,1,0:T(1,128)} copy(f32[5,16,1,1,512]{4,1,0,3,2:T(8,128)} %bitcast.1) | data formatting | bytes 327680
  45.3 1.4 %broadcast_multiply_fusion = f32[80,80]{1,0:T(8,128)} fusion(f32[80,80]{1,0:T(8,128)} %get-tuple-element.5), kind=kLoop, calls=%fused_computation | loop fusion | flops 6400 | bytes 51200 | tf_op jit(solution)/shard_map/mul | solution.py:421

commit v10 on v7

--- a/solution.py
+++ b/solution.py
@@ -67,7 +67,8 @@
             action(jnp.where(other >= devices, other - devices, other))
             return carry
 
-        lax.fori_loop(1, devices, step, 0, unroll=devices <= 64)
+        lax.fori_loop(members, devices, step, 0, unroll=devices <= 64)
+        lax.fori_loop(1, members, step, 0, unroll=devices <= 64)
 
     near_others = [lax.rem(member + o, members) for o in range(1, members)]
     near_peers = [plane * members + o for o in near_others]
@@ -213,7 +214,7 @@
         ] if level > 0 else []
         pending += ups + diags
         if level > 0:
-            part = coarse_part(packed)
+            send_coarse(level, coarse_part(packed))
         else:
             own = rows_c.at[me]
             to_all(lambda peer: send(own, own, rows_send, rows_recv, peer))
@@ -249,9 +250,7 @@
             weight_high, weight_rest = split(weight)
             load_high[...] = jnp.concatenate([weight_high] * pack, axis=0)
             load_rest[...] = jnp.concatenate([weight_rest] * pack, axis=0)
-            part = coarse_part(packed)
-        send_coarse(level, part)
-        if level == 0:
+            send_coarse(level, coarse_part(packed))
             for copy in ups:
                 copy.wait_recv()
             low_sub, low_grp = up_in[level, 0], up_in[level, 1]

time: 46.8 us -> 47.5 us (1.015)
  Pallas kernels: 42.9 us -> 43.6 us
    pallas_call x1, Pallas kernels: 42.9 us -> 43.6 us  [body(): pl.pallas_call(functools.partial(kernel, nsub, ngrp, inner, pack), out_sh...]
where the time goes in v10:
time: 47.5 us; the launch traced here: 47.3 us
  Pallas kernels  43.6 us (92%)
  local copies, waits for them, and re-layouts  2.99 us (6%)
  between operations  0.64 us (1%)
    pallas_call x1, Pallas kernels, body(): pl.pallas_call(functools.partial(kernel, nsub, ngrp, inner, pack), out_sh...  43.6 us
    unnamed x2, local copies, waits for them, and re-layouts  2.99 us

profile of v10, /device:TPU:0, one launch (start us, length us, event | category | flops | bytes accessed | tf_op | source)
XLA Modules:
  0.0 47.3 jit_solution(5119416900561759310)
XLA Ops:
  0.6 43.6 %shard_map.77 = (f32[5,16,1,1,512]{4,3,2,1,0:T(1,128)}, f32[80,80]{1,0:T(8,128)}) custom-call(f32[2]{0:T(128)} %bounds_hbm.1, f32[16,1,1,512]{3,2,1,0:T(1,128)} %res_hbm.1, bf16[1,1,1024,1024]{3,2,1,0:T(8,128)(2,1)} %inv_hbm.1, bf16[1,1,24,1024]{3,2,1,0:T(8,128)(2,1)} %corner_hbm.1, s32[1,1,24]{2,1,0:T(1,128)} %map_hbm.1, f32[1,32]{1,0:T(1,128)} %coarse_hbm.1), custom_call_target="tpu_custom_call" | custom-call | tf_op jit(solution)/shard_map/pallas_call | solution.py:351
  44.3 1.6 %copy.10 = f32[5,16,1,1,512]{4,3,2,1,0:T(1,128)} copy(f32[5,16,1,1,512]{4,3,2,1,0:T(1,128)} %get-tuple-element.4) | data formatting | bytes 327680
  45.9 1.4 %copy.11 = f32[80,80]{1,0:T(8,128)} copy(f32[80,80]{1,0:T(8,128)} %get-tuple-element.5) | data formatting | bytes 51200

commit v11 on v7

--- a/solution.py
+++ b/solution.py
@@ -212,9 +212,7 @@
             for d, peer in enumerate(diagonal_peers)
         ] if level > 0 else []
         pending += ups + diags
-        if level > 0:
-            part = coarse_part(packed)
-        else:
+        if level == 0:
             own = rows_c.at[me]
             to_all(lambda peer: send(own, own, rows_send, rows_recv, peer))
             loads[5].wait()
@@ -240,6 +238,7 @@
         first_low, second_low = own_part(face), own_part(3 * face)
         if level > 0:
             lows = send_lows(first_low, second_low)
+            part = coarse_part(packed)
         else:
             for copy in term_copies:
                 copy.wait_recv()

time: 46.8 us -> 46.7 us (level)
  no operation moved by 1% of the time
where the time goes in v11:
time: 46.7 us; the launch traced here: 46.5 us
  Pallas kernels  42.8 us (92%)
  local copies, waits for them, and re-layouts  2.99 us (6%)
  between operations  0.64 us (1%)
    pallas_call x1, Pallas kernels, body(): pl.pallas_call(functools.partial(kernel, nsub, ngrp, inner, pack), out_sh...  42.8 us
    unnamed x2, local copies, waits for them, and re-layouts  2.99 us

profile of v11, /device:TPU:0, one launch (start us, length us, event | category | flops | bytes accessed | tf_op | source)
XLA Modules:
  0.0 46.5 jit_solution(11821944521292204105)
XLA Ops:
  0.6 42.8 %shard_map.77 = (f32[5,16,1,1,512]{4,3,2,1,0:T(1,128)}, f32[80,80]{1,0:T(8,128)}) custom-call(f32[2]{0:T(128)} %bounds_hbm.1, f32[16,1,1,512]{3,2,1,0:T(1,128)} %res_hbm.1, bf16[1,1,1024,1024]{3,2,1,0:T(8,128)(2,1)} %inv_hbm.1, bf16[1,1,24,1024]{3,2,1,0:T(8,128)(2,1)} %corner_hbm.1, s32[1,1,24]{2,1,0:T(1,128)} %map_hbm.1, f32[1,32]{1,0:T(1,128)} %coarse_hbm.1), custom_call_target="tpu_custom_call" | custom-call | tf_op jit(solution)/shard_map/pallas_call | solution.py:351
  43.5 1.6 %copy.10 = f32[5,16,1,1,512]{4,3,2,1,0:T(1,128)} copy(f32[5,16,1,1,512]{4,3,2,1,0:T(1,128)} %get-tuple-element.4) | data formatting | bytes 327680
  45.1 1.4 %copy.11 = f32[80,80]{1,0:T(8,128)} copy(f32[80,80]{1,0:T(8,128)} %get-tuple-element.5) | data formatting | bytes 51200
